TPU v7x, 32 devices: a whole 2x2x4 slice. The times are simulated.
32 devices in a mesh: dp: 8 (over z, core), expert: 4 (over y, x).
Axes of the slice: x: 2, y: 2, z: 4, core: 2. Of those that a mesh axis runs over, the one named last changes fastest.
Arguments:
- features: bfloat16 [1024, 1024], P('dp'), may hold values from -6 to 6
- cross_weight: bfloat16 [1, 1024, 1024], replicated, may hold values from -0.1875 to 0.1875
- cross_bias: float32 [1, 1024], replicated, may hold values from -3 to 3
- gate_weight: bfloat16 [1024, 64], replicated, may hold values from -0.1875 to 0.1875
- gate_offset: float32 [64], replicated, may hold values from -3 to 3
- up_weight: bfloat16 [16, 1024, 8192], P('expert', None, 'dp'), may hold values from -0.1875 to 0.1875
- down_weight: bfloat16 [16, 8192, 1024], P('expert', 'dp'), may hold values from -0.0625 to 0.0625
- task_grad: bfloat16 [1024, 4, 1024], P('dp'), may hold values from -6 to 6
Outputs:
- task_mixed: bfloat16 [1024, 4, 1024], P('dp')
- feature_grad: bfloat16 [1024, 1024], P('dp')
- up_grad: bfloat16 [16, 1024, 8192], P('expert', None, 'dp')
- down_grad: bfloat16 [16, 8192, 1024], P('expert', 'dp')
- cross_grad: float32 [1, 1024, 1024], replicated
- bias_grad: float32 [1, 1024], replicated
- gating_grad: float32 [1024, 64], replicated
- offset_grad: float32 [64], replicated
All inputs are finite; a program needn't handle non-finite values.
Results may differ from a plain program's by a relative error of at most 0.012.
Values may be sent and summed in bfloat16 or wider, within the bound.
No kernel may reach another device: no remote copies, remote signals or barrier semaphores. Data moves between devices by JAX's collectives and lax.ppermute only.
A program may use at most 192 MiB of HBM per device.

v0:
```python
import functools
import itertools

import jax
import jax.numpy as jnp
from jax import lax
from jax.experimental import pallas as pl
from jax.experimental.pallas import tpu as pltpu
from jax.sharding import PartitionSpec as P

F32 = jnp.float32
BF16 = jnp.bfloat16
NN = (((1,), (0,)), ((), ()))
NT = (((1,), (1,)), ((), ()))
TN = (((0,), (0,)), ((), ()))
VMEM_LIMIT = 56 * 2**20
BACKWARD_PARTS = 1


def mm(a, b, dims=NN):
    return lax.dot_general(a, b, dims, preferred_element_type=F32)


def exact(values, ones):
    high = values.astype(BF16)
    low = (values - high.astype(F32)).astype(BF16)
    return mm(high, ones) + mm(low, ones)


def shift(values, size):
    assert size & (size - 1) == 0
    return lax.shift_right_logical(values, jnp.int32(size.bit_length() - 1))


def group_sum(values, experts):
    n = values.shape[1]
    row = shift(lax.broadcasted_iota(jnp.int32, (n, n), 0), experts)
    lane = shift(lax.broadcasted_iota(jnp.int32, (n, n), 1), experts)
    return exact(values, jnp.where(row == lane, 1.0, 0.0).astype(BF16))


def params(flops, name):
    return dict(
        compiler_params=pltpu.CompilerParams(vmem_limit_bytes=VMEM_LIMIT),
        cost_estimate=pl.CostEstimate(flops=flops, bytes_accessed=2**24, transcendentals=0),
        name=name,
    )


def cross_kernel(experts, n, *refs):
    feats, (cw_ref, cb_ref, gw_ref, go_ref) = refs[: 2 * n], refs[2 * n : 2 * n + 4]
    every_ref, shared_ref, gates_ref = refs[-3:]
    block = feats[0].shape[0]

    def half(feats):
        base = jnp.concatenate([f[...] for f in feats], axis=0)
        part = pl.ds(0, n * block)
        every_ref[part, :] = base
        wide = base.astype(F32)
        update = mm(base, cw_ref[...]) + cb_ref[...]
        shared = (wide * update + wide).astype(BF16)
        shared_ref[part, :] = shared
        expo = jnp.exp(mm(shared, gw_ref[...], NT) + go_ref[...])
        gates_ref[part, :] = expo / group_sum(expo, experts)

    pl.when(pl.program_id(0) == 0)(lambda: half(feats[:n]))
    pl.when(pl.program_id(0) == 1)(lambda: half(feats[n:]))


def cross(feats, cw, cb, gw, go, blocks, begin, before, tasks):
    block, d = feats[0].shape
    n = len(feats) // 2
    rows = 2 * blocks * block
    cols = gw.shape[0]
    vmem = pl.BlockSpec(memory_space=pltpu.VMEM)
    size = blocks if begin == 0 else n
    place = lambda i: ((i * blocks + begin) // size, 0)
    return pl.pallas_call(
        functools.partial(cross_kernel, cols // tasks, n),
        grid=(2,),
        in_specs=[vmem] * (len(feats) + 4) + [pl.BlockSpec(memory_space=pl.ANY) for _ in before],
        out_specs=[
            pl.BlockSpec((size * block, d), place),
            pl.BlockSpec((size * block, d), place),
            pl.BlockSpec((size * block, cols), place),
        ],
        out_shape=[
            jax.ShapeDtypeStruct((rows, d), BF16),
            jax.ShapeDtypeStruct((rows, d), BF16),
            jax.ShapeDtypeStruct((rows, cols), F32),
        ],
        input_output_aliases={len(feats) + 4 + k: k for k in range(len(before))},
        **params(n * 4 * block * d * d, "cross"),
    )(*feats, cw, cb, gw, go, *before)


def forward_kernel(shared_ref, up_ref, down_ref, *refs):
    act_ref, slope_ref, out_ref = refs[-3:]
    pre = mm(shared_ref[...], up_ref[0])
    sig = jax.nn.sigmoid(pre)
    act = pre * sig
    low = act.astype(BF16)
    act_ref[0] = low
    slope_ref[0] = (sig + act * (1.0 - sig)).astype(BF16)
    out_ref[0] = mm(low, down_ref[0]).astype(BF16)


def forward(shared, up, down, begin, count, before):
    rows, d = shared.shape
    local, _, hid = up.shape
    sub = min(rows, 512)
    here = lambda e, r: (begin + e, r, 0)
    there = lambda e, r: (begin + e, 0, 0)
    wide = jax.ShapeDtypeStruct((local, rows, hid), BF16)
    return pl.pallas_call(
        forward_kernel,
        grid=(count, rows // sub),
        in_specs=[
            pl.BlockSpec((sub, d), lambda e, r: (r, 0)),
            pl.BlockSpec((1, d, hid), there),
            pl.BlockSpec((1, hid, d), there),
        ]
        + [pl.BlockSpec(memory_space=pl.ANY) for _ in before],
        out_specs=[
            pl.BlockSpec((1, sub, hid), here),
            pl.BlockSpec((1, sub, hid), here),
            pl.BlockSpec((1, sub, d), here),
        ],
        out_shape=[wide, wide, jax.ShapeDtypeStruct((local, rows, d), BF16)],
        input_output_aliases={3 + k: k for k in range(len(before))},
        **params(4 * rows * d * hid * count, "forward"),
    )(shared, up, down, *before)


def same_row(n, m, group):
    row = lax.broadcasted_iota(jnp.int32, (n, m), 0) & (group - 1)
    lane = lax.broadcasted_iota(jnp.int32, (1, m), 1) & (group - 1)
    return jnp.where(row == lane, 1.0, 0.0)


def chosen(ids_ref, order, by_task, tasks, local, experts, cols, group):
    wide = tasks * local * group
    lane = shift(lax.broadcasted_iota(jnp.int32, (1, wide), 1), group)
    task = shift(lane, local) if by_task else lane & (tasks - 1)
    expert = lane & (local - 1) if by_task else shift(lane, tasks)
    ids = jnp.zeros_like(lane) + ids_ref[order]
    for t in range(1, tasks):
        ids = jnp.where(task == t, ids_ref[order + t], ids)
    row = lax.broadcasted_iota(jnp.int32, (cols, wide), 0)
    return jnp.where(row == ids * experts + ids_ref[0] + expert, 1.0, 0.0).astype(BF16)


def stack(weights, r, group, count, width):
    return jnp.concatenate(
        [weights[r : r + group, j * width : (j + 1) * width] for j in range(count)], axis=0
    )


def mix_kernel(tasks, experts, block, ids_ref, gates_ref, outs_ref, keep_ref, send_ref):
    i = pl.program_id(0)
    rows, cols = gates_ref.shape
    local = outs_ref.shape[0]
    group = 256 // local
    flat = same_row(block, tasks * local * group, group)
    step = rows // block

    def write(ref):
        for k in range(step):
            at = pl.ds(k * block, block)
            order = 1 + 2 * tasks * (i * step + k) + tasks
            weights = mm(
                gates_ref[at, :].astype(BF16),
                chosen(ids_ref, order, True, tasks, local, experts, cols, group),
            )
            weights = (weights * flat).astype(BF16)
            for r in range(0, block, group):
                part = pl.ds(k * block + r, group)
                out = jnp.concatenate([outs_ref[j, part, :] for j in range(local)], axis=0)
                both = mm(stack(weights, r, group, tasks, local * group), out).astype(BF16)
                for t in range(tasks):
                    ref[t, part, :] = both[t * group : (t + 1) * group]

    pl.when(i < pl.num_programs(0) // 2)(lambda: write(keep_ref))
    pl.when(i >= pl.num_programs(0) // 2)(lambda: write(send_ref))


def mix(ids, gates, outs, n, tasks):
    local, rows, d = outs.shape
    cols = gates.shape[1]
    sub = rows // 4
    return pl.pallas_call(
        functools.partial(mix_kernel, tasks, cols // tasks, rows // n),
        grid_spec=pltpu.PrefetchScalarGridSpec(
            num_scalar_prefetch=1,
            grid=(4,),
            in_specs=[
                pl.BlockSpec((sub, cols), lambda i, f: (i, 0)),
                pl.BlockSpec((local, sub, d), lambda i, f: (0, i, 0)),
            ],
            out_specs=[
                pl.BlockSpec((tasks, sub, d), lambda i, f: (0, jnp.minimum(i, 1), 0)),
                pl.BlockSpec((tasks, sub, d), lambda i, f: (0, jnp.maximum(i - 2, 0), 0)),
            ],
        ),
        out_shape=[jax.ShapeDtypeStruct((tasks, rows // 2, d), BF16)] * 2,
        **params(2**11 * rows * d, "mix"),
    )(ids, gates, outs)


def spread_kernel(tasks, experts, places, n_grads, begin, ids_ref, *refs):
    grads = refs[:n_grads]
    gates_ref, outs_ref = refs[n_grads : n_grads + 2]
    og_ref, inner_ref, rows_ref, sems = refs[-4:]
    i = pl.program_id(0)
    rows, cols = gates_ref.shape
    count = rows_ref.shape[1]
    block = rows // count
    local = og_ref.shape[0]
    group = 256 // local

    def fetch(step, slot, act):
        for k in range(len(places) // count):

            @pl.when(step == k)
            def _():
                for j in range(count):
                    for t, (which, *lead) in enumerate(places[k * count + j]):
                        act(
                            pltpu.make_async_copy(
                                grads[which].at[tuple(lead)],
                                rows_ref.at[slot, j, t],
                                sems.at[slot, j, t],
                            )
                        )

    @pl.when(i == 0)
    def _():
        fetch(0, 0, lambda copy: copy.start())

    fetch(i + 1, (i + 1) & 1, lambda copy: copy.start())
    flat = same_row(block, tasks * local * group, group)
    square = same_row(tasks * group, local * group, group)
    fetch(i, i & 1, lambda copy: copy.wait())
    slot = i & 1
    for k in range(count):
        order = 1 + 2 * tasks * ((begin + i) * count + k)
        at = pl.ds(k * block, block)
        gates = gates_ref[at, :]
        pick = lambda by_task: chosen(
            ids_ref, order, by_task, tasks, local, experts, cols, group
        )
        weights = (mm(gates.astype(BF16), pick(False)) * flat).astype(BF16)
        inners = []
        for r in range(0, block, group):
            part = pl.ds(k * block + r, group)
            grad = jnp.concatenate(
                [rows_ref[slot, k, t, r : r + group, :] for t in range(tasks)], axis=0
            )
            out = jnp.concatenate([outs_ref[j, part, :] for j in range(local)], axis=0)
            both = mm(stack(weights, r, group, local, tasks * group), grad).astype(BF16)
            for j in range(local):
                og_ref[j, part, :] = both[j * group : (j + 1) * group]
            products = mm(grad, out, NT) * square
            inners.append(
                jnp.concatenate(
                    [products[t * group : (t + 1) * group] for t in range(tasks)], axis=1
                )
            )
        inner = jnp.concatenate(inners, axis=0)
        high = inner.astype(BF16)
        rest = (inner - high.astype(F32)).astype(BF16)
        at_column = pick(True)
        inner_ref[at, :] = mm(high, at_column, NT) + mm(rest, at_column, NT)


def spread_grads(ids, grads, places, gates, outs, begin, before, tasks):
    local, rows, d = outs.shape
    cols = gates.shape[1]
    n = len(places)
    count = 1
    block = rows // 2 // n
    sub = count * block
    begin = begin * (n // count)
    every = lambda i, f: (0, begin + i, 0)
    here = lambda i, f: (begin + i, 0)
    return pl.pallas_call(
        functools.partial(spread_kernel, tasks, cols // tasks, places, len(grads), begin),
        grid_spec=pltpu.PrefetchScalarGridSpec(
            num_scalar_prefetch=1,
            grid=(n // count,),
            in_specs=[pl.BlockSpec(memory_space=pl.ANY) for _ in grads]
            + [pl.BlockSpec((sub, cols), here), pl.BlockSpec((local, sub, d), every)]
            + [pl.BlockSpec(memory_space=pl.ANY) for _ in before],
            out_specs=[
                pl.BlockSpec((local, sub, d), every),
                pl.BlockSpec((sub, cols), here),
            ],
            scratch_shapes=[
                pltpu.VMEM((2, count, tasks, block, d), BF16),
                pltpu.SemaphoreType.DMA((2, count, tasks)),
            ],
        ),
        out_shape=[
            jax.ShapeDtypeStruct((local, rows, d), BF16),
            jax.ShapeDtypeStruct((rows, cols), F32),
        ],
        input_output_aliases={3 + len(grads) + k: k for k in range(len(before))},
        **params(2**10 * rows * d, "spread_grads"),
    )(ids, *grads, gates, outs, *before)


def backward_kernel(tasks, experts, n, sub, start, last, ids_ref, *refs):
    og_ref, slope_ref, up_ref, down_ref = refs[:4]
    total_ref = None if start else refs[4]
    if last:
        gates_ref, inner_ref = refs[5 - start : 7 - start]
        pg_ref, keep_ref, send_ref, acc_ref, pair_ref = refs[-5:]
    else:
        pg_ref, acc_ref = refs[-2:]
    e = pl.program_id(0)
    rows, d = acc_ref.shape

    for r in range(0, rows, sub):
        part = pl.ds(r, sub)
        hidden = mm(og_ref[0, part, :], down_ref[0], NT)
        pre_grad = (hidden * slope_ref[0, part, :].astype(F32)).astype(BF16)
        pg_ref[0, part, :] = pre_grad
        found = mm(pre_grad, up_ref[0], NT)

        @pl.when(e == 0)
        def _():
            acc_ref[part, :] = found if start else total_ref[part, :] + found

        @pl.when(e > 0)
        def _():
            acc_ref[part, :] += found

    if not last:
        return
    cols = gates_ref.shape[1]
    block = rows // n
    quarter = block // tasks

    @pl.when(e == 0)
    def _():
        gates, inner = gates_ref[...], inner_ref[...]
        logit = gates * (inner - group_sum(gates * inner, experts))
        high = logit.astype(BF16)
        rest = (logit - high.astype(F32)).astype(BF16)
        row = lax.broadcasted_iota(jnp.int32, (cols, 2 * cols), 0)
        lane = lax.broadcasted_iota(jnp.int32, (cols, 2 * cols), 1)
        one = jnp.where(lane == row, 1.0, 0.0).astype(BF16)
        two = jnp.where(lane == row + cols, 1.0, 0.0).astype(BF16)
        pair_ref[...] = (mm(high, one) + mm(rest, two)).astype(BF16)

    @pl.when(e == pl.num_programs(0) - 1)
    def _():
        for i in range(n):
            ref = keep_ref if i < n // 2 else send_ref
            for t in range(tasks):
                place = ids_ref[1 + 2 * tasks * i + tasks + t]
                begin = pl.multiple_of(i * block + place * quarter, quarter)
                source = pl.ds(begin, quarter)
                dest = pl.ds(i % (n // 2) * quarter, quarter)
                ref[t, dest, :d] = acc_ref[source, :].astype(BF16)
                ref[t, dest, d:] = pair_ref[source, :]


def backward(ids, og, slope, up, down, gates, inner, n, begin, count, before, last, tasks):
    local, rows, d = og.shape
    hid = up.shape[2]
    here = lambda e, f: (begin + e, 0, 0)
    cols = gates.shape[1]
    width = d + 2 * cols
    packed = (tasks, rows // 2 // tasks, width)
    start = before is None
    whole = lambda shape, **how: pl.BlockSpec(shape, lambda e, f: (0,) * len(shape), **how)
    specs, shapes, scratch = [whole((rows, d))], [jax.ShapeDtypeStruct((rows, d), F32)], []
    if last:
        specs, shapes = [whole(packed)] * 2, [jax.ShapeDtypeStruct(packed, BF16)] * 2
        scratch = [pltpu.VMEM((rows, d), F32), pltpu.VMEM((rows, 2 * cols), BF16)]
    args, in_specs = [], []
    if not start:
        args, in_specs = [before[1]], [whole((rows, d), pipeline_mode=pl.Buffered(1))]
    if last:
        args, in_specs = args + [gates, inner], in_specs + [whole((rows, cols))] * 2
    if not start:
        args, in_specs = args + [before[0]], in_specs + [pl.BlockSpec(memory_space=pl.ANY)]
    return pl.pallas_call(
        functools.partial(
            backward_kernel, tasks, cols // tasks, n, min(rows, 512), start, last
        ),
        grid_spec=pltpu.PrefetchScalarGridSpec(
            num_scalar_prefetch=1,
            grid=(count,),
            in_specs=[
                pl.BlockSpec((1, rows, d), here),
                pl.BlockSpec((1, rows, hid), here),
                pl.BlockSpec((1, d, hid), here),
                pl.BlockSpec((1, hid, d), here),
            ]
            + in_specs,
            out_specs=[pl.BlockSpec((1, rows, hid), here)] + specs,
            scratch_shapes=scratch,
        ),
        out_shape=[jax.ShapeDtypeStruct((local, rows, hid), BF16)] + shapes,
        input_output_aliases={} if start else {4 + len(args): 0},
        **params(4 * rows * d * hid * count, "backward"),
    )(ids, og, slope, up, down, *args)


def weights_kernel(n, *refs):
    shared, acts, ogs, pgs = (refs[k * n : (k + 1) * n] for k in range(4))
    up_ref, down_ref = refs[-2:]
    total = sum(mm(s[...], p[0], TN) for s, p in zip(shared, pgs))
    up_ref[0] = total.astype(BF16)
    total = sum(mm(a[0], o[0], TN) for a, o in zip(acts, ogs))
    down_ref[0] = total.astype(BF16)


def weight_grads(shared, acts, ogs, pgs, begin, count, before):
    local, rows, hid = acts[0].shape
    d = shared[0].shape[1]
    n = len(shared)
    there = lambda e, h: (begin + e, 0, 0)
    half = [pl.BlockSpec((1, x.shape[1], hid // 2), lambda e, h: (begin + e, 0, h)) for x in acts]
    return pl.pallas_call(
        functools.partial(weights_kernel, n),
        grid=(count, 2),
        in_specs=[pl.BlockSpec(s.shape, lambda e, h: (0, 0)) for s in shared]
        + half
        + [pl.BlockSpec((1,) + x.shape[1:], there) for x in ogs]
        + half
        + [pl.BlockSpec(memory_space=pl.ANY) for _ in before],
        out_specs=[
            pl.BlockSpec((1, d, hid // 2), lambda e, h: (begin + e, 0, h)),
            pl.BlockSpec((1, hid // 2, d), lambda e, h: (begin + e, h, 0)),
        ],
        out_shape=[
            jax.ShapeDtypeStruct((local, d, hid), BF16),
            jax.ShapeDtypeStruct((local, hid, d), BF16),
        ],
        input_output_aliases={4 * n + k: k for k in range(len(before))},
        **params(4 * n * rows * d * hid * count, "weight_grads"),
    )(*shared, *acts, *ogs, *pgs, *before)


def rows_kernel(tasks, cols, bases, sizes, ids_ref, *refs):
    n = len(bases)
    parts, pairs = refs[:n], refs[n : 2 * n]
    feat_ref, tile_ref, shared_ref = refs[2 * n : 2 * n + 3]
    cross_ref, bias_ref, gating_ref, offset_ref, every_ref, pair_ref = refs[2 * n + 3 :]
    for k, (base, (half, slot)) in enumerate(zip(bases, sizes)):
        shares, blocks, quarter, _ = parts[k].shape
        block = quarter * tasks
        for s in range(shares):
            place = ids_ref[1 + (2 - half) * tasks + slot + s] * quarter
            for j in range(blocks):
                rows = pl.ds(pl.multiple_of(base + j * block + place, quarter), quarter)
                every_ref[rows, :] = parts[k][s, j]
                pair_ref[rows, :] = pairs[k][s, j]
    scaled = (every_ref[...].astype(F32) * tile_ref[...].astype(F32)).astype(BF16)
    cross_ref[...] = mm(feat_ref[...], scaled, TN)
    bias_ref[...] = jnp.sum(scaled.astype(F32), axis=0, keepdims=True)
    pair = pair_ref[...]
    gating_ref[...] = mm(pair[:, :cols], shared_ref[...], TN)
    offset = jnp.sum(pair.astype(F32), axis=0, keepdims=True)
    offset_ref[...] = offset[:, :cols] + offset[:, cols:]


def rows_grads(ids, found, feat, shared, cols, tasks):
    rows, d = feat.shape
    tile = 512
    parts, bases, sizes = [], [], []
    for half, (base, some) in enumerate(found):
        slot = 0
        for part in some:
            parts.append(part)
            bases.append(base)
            sizes.append((half % 2, slot))
            slot += part.shape[0]
    wide = parts[0].shape[-1] - d
    column = lambda j: (0, j)
    return pl.pallas_call(
        functools.partial(rows_kernel, tasks, cols, bases, sizes),
        grid=(d // tile,),
        in_specs=[pl.BlockSpec(memory_space=pltpu.SMEM)]
        + [pl.BlockSpec(p.shape[:3] + (tile,), lambda j: (0, 0, 0, j)) for p in parts]
        + [pl.BlockSpec(p.shape[:3] + (wide,), lambda j: (0, 0, 0, d // wide)) for p in parts]
        + [
            pl.BlockSpec((rows, d), lambda j: (0, 0), pipeline_mode=pl.Buffered(1)),
            pl.BlockSpec((rows, tile), column),
            pl.BlockSpec((rows, tile), column),
        ],
        out_specs=[
            pl.BlockSpec((d, tile), column),
            pl.BlockSpec((1, tile), column),
            pl.BlockSpec((cols, tile), column),
            pl.BlockSpec((1, cols), lambda j: (0, 0)),
        ],
        out_shape=[
            jax.ShapeDtypeStruct((d, d), F32),
            jax.ShapeDtypeStruct((1, d), F32),
            jax.ShapeDtypeStruct((cols, d), F32),
            jax.ShapeDtypeStruct((1, cols), F32),
        ],
        scratch_shapes=[pltpu.VMEM((rows, tile), BF16), pltpu.VMEM((rows, wide), BF16)],
        **params(2 * rows * d * d, "rows_grads"),
    )(ids, *parts, *parts, feat, feat, shared)


def added(parts):
    return sum(p.astype(F32) for p in parts)


class Ring:
    def __init__(self, dp, expert):
        size = dp * expert

        def pairs(move):
            found = []
            for i in range(size):
                z, c, q = i // expert // 2, i // expert % 2, i % expert
                z, c, q = move(z, c, q)
                found.append((i, (z * 2 + c) * expert + q))
            return found

        self.core_pairs = pairs(lambda z, c, q: (z, 1 - c, q))
        self.z1_pairs = pairs(lambda z, c, q: (z ^ 1, c, q))
        self.z3_pairs = pairs(lambda z, c, q: (z ^ 3, c, q))
        self.e1_pairs = pairs(lambda z, c, q: (z, c, q ^ (1, 2)[c]))
        self.e2_pairs = pairs(lambda z, c, q: (z, c, q ^ (2, 1)[c]))

        places = [tuple((0, t) for t in range(4))]
        for k, j in ((1, 0), (4, 0), (4, 1)):
            places.append(((k, 0, j), (k + 1, 0, j), (k + 2, 0, j), (k + 2, 1, j)))
        self.places, self.blocks = tuple(places), 8

    def move(self, x, pairs):
        return lax.ppermute(x, ("dp", "expert"), pairs)

    def core(self, x):
        return self.move(x, self.core_pairs)

    def orders(self):
        q, c = lax.axis_index("expert"), lax.axis_index("dp") % 2
        b1, b2 = 1 + c, 2 - c
        return [q, q ^ b2, q ^ b1, q ^ 3], [q, q ^ b1, q ^ b2, q ^ 3]

    def ids(self, first, tasks):
        mine, other = self.orders()
        plain = list(range(tasks))
        ids = [first]
        for order in (mine, other):
            for k in range(4):
                ids += plain if k == 0 else (other if order is mine else mine)
                ids += order
        return [jnp.stack([jnp.asarray(i, jnp.int32) for i in ids])]

    def spread(self, x):
        one = self.move(x, self.e1_pairs)
        rest = self.move(jnp.stack([x, one]), self.e2_pairs)
        return x[None], one[None], rest

    def in_order(self, parts, order):
        parts = jnp.concatenate(parts, axis=0)
        place = lambda share: sum(jnp.where(order[i] == share, i, 0) for i in range(4))
        return [lax.dynamic_index_in_dim(parts, place(i), 0, False) for i in range(4)]

    def rows(self, x):
        three, one = self.move(x, self.z3_pairs), self.move(x, self.z1_pairs)
        three, one = lax.optimization_barrier((three, one))
        mine = [x, three, one]
        last = self.move(three, self.z1_pairs)
        both = lambda parts: parts + [self.core(p) for p in parts]
        return [[both(mine), lambda *after: both([tie(last, *after)])]], one, last

    def grads(self, task_grad):
        own = jnp.transpose(task_grad, (1, 0, 2))
        share = lax.dynamic_index_in_dim(task_grad, lax.axis_index("expert"), 1, False)
        core, move = self.core, self.move
        share, own = yield (share, own)
        three, own2 = yield (move(share, self.z3_pairs), core(own))
        a0 = three[None]
        both, a0 = yield (jnp.stack([share, three]), a0)
        b0, a1 = yield (move(both, self.z1_pairs), move(a0, self.e1_pairs))
        b0, out = yield (b0, jnp.stack([a0, a1]))
        b1, a2 = yield (move(b0, self.e1_pairs), move(out, self.e2_pairs))
        out, *a = yield (jnp.stack([b0, b1]), a0, a1, a2)
        b2, *other_a = yield (move(out, self.e2_pairs), *map(core, a))
        lift = lambda x, y, z: [x[None], y[None], z]
        self.near = [[own, *lift(*a), *lift(b0, b1, b2)]]
        b = yield (b0, b1, b2)
        other_b = yield tuple(map(core, b))
        far = [own2, *lift(*other_a), *lift(*other_b)]
        return self.near, [far], self.places

    def reduce(self, parts, scatter):
        ((keep, send),) = parts
        (out,) = yield (send,)
        (got,) = yield (self.core(out),)
        parts = [keep, got]
        (out,) = yield (added([p[2:] for p in parts]).astype(BF16),)
        (got,) = yield (self.move(out, self.e1_pairs),)
        parts = [p[:2] for p in parts] + [got]
        (out,) = yield (added([p[1] for p in parts]).astype(BF16),)
        (got,) = yield (self.move(out, self.e2_pairs),)
        parts = [p[0] for p in parts] + [got]
        half = got.shape[0] // 2
        if scatter:
            (out,) = yield (added([p[half:] for p in parts]).astype(BF16),)
            (got,) = yield (self.move(out, self.z1_pairs),)
            parts = [p[:half] for p in parts] + [got]
            half = half // 2
            (out,) = yield (added([p[half:] for p in parts]).astype(BF16),)
            (got,) = yield (self.move(out, self.z3_pairs),)
            return added([p[:half] for p in parts] + [got])
        shape = (4, -1, got.shape[-1])
        (out,) = yield (added(parts).astype(BF16).reshape(shape),)
        (got,) = yield (self.move(out, self.z1_pairs),)
        out = added([out, jnp.concatenate([got[2:], got[:2]], axis=0)])
        (out,) = yield (out.astype(BF16),)
        (got,) = yield (self.move(out, self.z3_pairs),)
        return added([out, jnp.stack([got[1], got[0], got[3], got[2]])])

    def share_tasks(self, x):
        return self.in_order(self.spread(x), self.orders()[1])

    def share_rows(self, x):
        mine = self.spread(x)
        own = jnp.concatenate(self.in_order([m[:, 0] for m in mine], self.orders()[1]), axis=0)
        other = [self.core(p) for p in mine]
        block = x.shape[1] * 4
        return [(0, mine), (4 * block, other)], own


class Steps:
    def __init__(self, steps):
        self.steps, self.moved, self.value = steps, None, None
        self.operand = self._next(None)

    def _next(self, sent):
        try:
            return self.steps.send(sent)
        except StopIteration as stop:
            self.value = stop.value

    def start(self, *after):
        if self.operand is not None:
            self.moved, self.operand = self._next(tie(self.operand, *after)), None

    def finish(self, *after):
        if self.moved is not None:
            moved, self.moved = self.moved, None
            self.operand = self._next(tie(moved, *after))

    def result(self):
        while self.moved is not None or self.operand is not None:
            self.start()
            self.finish()
        return self.value


def finish(steps, *after):
    moved = tie([s.moved or () for s in steps], *after)
    for one, arrays in zip(steps, moved):
        if one.moved is not None:
            one.moved = arrays
            one.finish()


def tie(x, *others):
    others = [o for o in others if o is not None]
    return lax.optimization_barrier((x, *others))[0] if others else x


class Plain:
    def __init__(self, dp, expert):
        self.dp = dp
        self.count = dp // 8 if dp % 8 == 0 else 1
        self.blocks = dp // self.count

    def ids(self, first, tasks):
        plain = list(range(tasks)) * 2 * self.blocks
        return [jnp.stack([jnp.asarray(i, jnp.int32) for i in (first, *plain)])] * self.count

    def rows(self, x):
        every = lax.all_gather(x, "dp", axis=0, tiled=True)
        blocks = jnp.split(every, self.dp)
        n = self.blocks
        return [[blocks[i : i + n]] for i in range(0, self.dp, n)], None, None

    def grads(self, task_grad):
        every = lax.all_gather(jnp.transpose(task_grad, (1, 0, 2)), "dp", axis=0)
        tasks, half = task_grad.shape[1], self.blocks // 2
        self.places = tuple(tuple((0, i, t) for t in range(tasks)) for i in range(half))
        parts = jnp.split(every, 2 * self.count)
        self.near = [[p] for p in parts[::2]]
        return self.near, [[p] for p in parts[1::2]], self.places
        yield

    def reduce(self, parts, scatter):
        blocks = []
        for part in (p for pair in parts for p in pair):
            part = part.reshape(part.shape[0], self.blocks // 2, -1, part.shape[-1])
            blocks.append(jnp.swapaxes(part.astype(F32), 0, 1))
        blocks = jnp.concatenate(blocks, axis=0)
        own = lax.psum_scatter(blocks, "dp", scatter_dimension=0, tiled=True)[0]
        return lax.psum(own, "expert")
        yield

    def share_tasks(self, x):
        return list(x)

    def share_rows(self, x):
        every = jnp.swapaxes(lax.all_gather(x, "dp", axis=0), 0, 1)
        shares, _, quarter, d = every.shape
        found = []
        for k, part in enumerate(jnp.split(every, 2 * self.count, axis=1)):
            found.append((k * self.blocks // 2 * quarter * shares, [part]))
        return found, x.reshape(-1, d)


def local_step(
    net, features, cross_weight, cross_bias, gate_weight, gate_offset, up_weight, down_weight,
    task_grad,
):
    block, d = features.shape
    tasks = task_grad.shape[1]
    cols = gate_weight.shape[1]
    local = up_weight.shape[0]
    first = lax.axis_index("expert") * local
    ids = net.ids(first, tasks)

    feats, early, late = net.rows(features)
    grads = Steps(net.grads(task_grad))
    grads.start(early)

    lowered = []
    for pieces in feats:
        found, begin = (), 0
        for piece in pieces:
            piece = piece(*found, grads.moved) if callable(piece) else piece
            found = cross(
                piece, cross_weight[0], cross_bias, gate_weight.T, gate_offset[None],
                net.blocks // 2, begin, found, tasks,
            )
            begin += len(piece) // 2
        lowered.append(found)
    feats, shared, gates = zip(*lowered)
    grads.finish(*shared)
    ready = grads.operand
    grads.start()
    done = [() for _ in shared]
    quarter = local // 4
    sizes = (local - 2 * quarter, quarter, quarter) if quarter else (local,)
    begins = list(itertools.accumulate((0, *sizes)))
    for b, size in zip(begins, sizes):
        if b:
            grads.finish(*[found[0] for found in done])
            ready = grads.operand
            grads.start()
        done = [
            forward(tie(low, ready), up_weight, down_weight, b, size, found)
            for low, found in zip(shared, done)
        ]
    acts, slopes, outs = zip(*done)
    grads.finish(*[found[0] for found in done])
    ready = grads.operand
    grads.start()
    n = net.blocks
    mixed = [mix(i, tie(gt, ready), o, n, tasks) for i, gt, o in zip(ids, gates, outs)]
    grads.finish(*[keep for keep, _ in mixed])
    near, places = net.near, net.places
    ready = grads.operand
    grads.start()
    mixed = Steps(net.reduce(mixed, True))
    mixed.start()
    spread = [
        spread_grads(i, g, places, tie(gt, ready), o, 0, (), tasks)
        for i, g, gt, o in zip(ids, near, gates, outs)
    ]
    finish([grads, mixed], *[og for og, _ in spread])
    far = grads.result()[1]
    spread = [
        spread_grads(i, g, places, gt, o, 1, tie(x, mixed.operand), tasks)
        for i, g, gt, o, x in zip(ids, far, gates, outs, spread)
    ]
    back = [None for _ in spread]
    parts = BACKWARD_PARTS if local % BACKWARD_PARTS == 0 else 1
    for k in range(parts):
        ready = mixed.operand
        mixed.start()
        back = [
            backward(
                i, tie(og, ready), slope, up_weight, down_weight, gt, inner, n,
                k * local // parts, local // parts, before, k == parts - 1, tasks,
            )
            for i, (og, inner), slope, gt, before in zip(ids, spread, slopes, gates, back)
        ]
        if k < parts - 1:
            mixed.finish(*[x[0] for x in back])
    ogs = [og for og, _ in spread]
    pgs = [b[0] for b in back]
    total = Steps(net.reduce(tie([b[1:] for b in back], mixed.moved), False))
    total.start()
    total.finish()
    mixed.finish(*pgs)
    weights = ()
    for b, size in zip(begins, sizes):
        ready = (mixed.operand, total.operand)
        total.start()
        mixed.start()
        tied = [tie(a, *ready) for a in acts]
        weights = weight_grads(shared, tied, ogs, pgs, b, size, weights)
        finish([total, mixed], weights[0])
    up_grad, down_grad = weights
    total = total.result()
    task_mixed = mixed.result().astype(BF16)
    task_mixed = jnp.stack(net.share_tasks(task_mixed), axis=1)

    logit = total[..., d : d + cols] + total[..., d + cols :]
    high = logit.astype(BF16)
    low = (logit - high.astype(F32)).astype(BF16)
    upstream = total[..., :d] + lax.dot_general(
        high, gate_weight, (((high.ndim - 1,), (1,)), ((), ())), preferred_element_type=F32
    )
    every, own = net.share_rows(jnp.concatenate([upstream.astype(BF16), high, low], axis=-1))
    feats, shared = (x[0] if len(x) == 1 else jnp.concatenate(x, axis=0) for x in (feats, shared))
    cross_grad, bias_grad, gating_grad, offset_grad = rows_grads(
        ids[0], every, feats, shared, cols, tasks
    )

    update = mm(features, cross_weight[0]) + cross_bias
    upstream = own[:, :d].astype(F32)
    scaled = (upstream * features.astype(F32)).astype(BF16)
    feature_grad = (upstream + mm(scaled, cross_weight[0], NT) + upstream * update).astype(BF16)
    return (
        task_mixed,
        feature_grad,
        up_grad,
        down_grad,
        cross_grad[None],
        bias_grad,
        gating_grad.T,
        offset_grad[0],
    )


def solution(mesh):
    dp, expert = mesh.shape["dp"], mesh.shape["expert"]
    net = (Ring if (dp, expert) == (8, 4) else Plain)(dp, expert)
    return jax.shard_map(
        functools.partial(local_step, net),
        mesh=mesh,
        in_specs=(
            P("dp", None),
            P(),
            P(),
            P(),
            P(),
            P("expert", None, "dp"),
            P("expert", "dp", None),
            P("dp", None, None),
        ),
        out_specs=(
            P("dp", None, None),
            P("dp", None),
            P("expert", None, "dp"),
            P("expert", "dp", None),
            P(),
            P(),
            P(),
            P(),
        ),
        check_vma=False,
    )
```

profile of v0, /device:TPU:0, one launch (start us, length us, event | category | flops | bytes accessed | tf_op | source)
XLA Modules:
  0.0 249.4 jit_solution(7473648276619328444)
XLA Ops:
  0.6 5.1 %collective-permute-start = (bf16[128,1024]{1,0:T(8,128)(2,1)}, bf16[128,1024]{1,0:T(8,128)(2,1)S(1)}, u32[]{:S(2)}, u32[]{:S(2)}) collective-permute-start(bf16[128,1024]{1,0:T(8,128)(2,1)} %refs_0_.1), channel_id=1, source_target_pairs={{0,24},{1,25},{2,26},{3,27},{4,28},{5,29},{6,30},{7,31},{8,16},{9,... | collective-permute-start | bytes 786440 | tf_op jit(solution)/shard_map/ppermute | solution.py:540
  7.3 5.9 %collective-permute-done.refs_1_ = bf16[128,1024]{1,0:T(8,128)(2,1)S(1)} collective-permute-done((bf16[128,1024]{1,0:T(8,128)(2,1)}, bf16[128,1024]{1,0:T(8,128)(2,1)S(1)}, u32[]{:S(2)}, u32[]{:S(2)}) %collective-permute-start) | collective-permute-done | bytes 262176 | tf_op jit(solution)/shard_map/ppermute | solution.py:540
  13.2 4.8 %collective-permute-done.1.refs_2_ = bf16[128,1024]{1,0:T(8,128)(2,1)S(1)} collective-permute-done((bf16[128,1024]{1,0:T(8,128)(2,1)}, bf16[128,1024]{1,0:T(8,128)(2,1)S(1)}, u32[]{:S(2)}, u32[]{:S(2)}) %collective-permute-start.1) | collective-permute-done | bytes 262176 | tf_op jit(solution)/shard_map/ppermute | solution.py:540
  23.7 6.6 %cross.2 = (bf16[1024,1024]{1,0:T(8,128)(2,1)}, bf16[1024,1024]{1,0:T(8,128)(2,1)}, f32[1024,64]{1,0:T(8,128)}) custom-call(bf16[128,1024]{1,0:T(8,128)(2,1)} %refs_0_.1, bf16[128,1024]{1,0:T(8,128)(2,1)} %copy-done.24, bf16[128,1024]{1,0:T(8,128)(2,1)} %copy-done.25, bf16[128,1024]{1,0:T(8,128)(2,1)} %copy-done.26, bf16[128,1024]{1,0:T(8,128)(2,1)} %copy-done.27, ...), custom_call_target="tpu_custom_call" | custom-call | flops 1610612736 | bytes 16777216 | tf_op jit(solution)/shard_map/cross/pallas_call | solution.py:78
  30.4 4.4 %collective-permute-done.2.refs_0_ = bf16[128,1024]{1,0:T(8,128)(2,1)S(1)} collective-permute-done((bf16[128,1024]{1,0:T(8,128)(2,1)S(1)}, bf16[128,1024]{1,0:T(8,128)(2,1)S(1)}, u32[]{:S(2)}, u32[]{:S(2)}) %collective-permute-start.2) | collective-permute-done | bytes 262176 | tf_op jit(solution)/shard_map/ppermute | solution.py:540
  37.1 4.2 %cross.3 = (bf16[1024,1024]{1,0:T(8,128)(2,1)}, bf16[1024,1024]{1,0:T(8,128)(2,1)}, f32[1024,64]{1,0:T(8,128)}) custom-call(bf16[128,1024]{1,0:T(8,128)(2,1)} %copy-done.20, bf16[128,1024]{1,0:T(8,128)(2,1)} %copy-done.21, bf16[1024,1024]{1,0:T(8,128)(2,1)} %bitcast.90, ...), custom_call_target="tpu_custom_call", output_to_operand_aliasing={{0}: (6, {}), {1}: (7, {}), {2}: (8, {})} | custom-call | flops 536870912 | bytes 16777216 | tf_op jit(solution)/shard_map/cross/pallas_call | solution.py:78
  43.0 14.8 %forward.3 = (bf16[4,1024,1024]{2,1,0:T(8,128)(2,1)}, bf16[4,1024,1024]{2,1,0:T(8,128)(2,1)}, bf16[4,1024,1024]{2,1,0:T(8,128)(2,1)}) custom-call(bf16[1024,1024]{1,0:T(8,128)(2,1)} %get-tuple-element.101.shared_ref.refs_0_.refs_14_, bf16[4,1024,1024]{2,1,0:T(8,128)(2,1)} %refs_2_.1, bf16[4,1024,1024]{2,1,0:T(8,128)(2,1)} %refs_3_.3), custom_call_target="tpu_custom_call" | custom-call | flops 8589934592 | bytes 16777216 | tf_op jit(solution)/shard_map/forward/pallas_call | solution.py:115
  60.0 8.6 %forward.4 = (bf16[4,1024,1024]{2,1,0:T(8,128)(2,1)}, bf16[4,1024,1024]{2,1,0:T(8,128)(2,1)}, bf16[4,1024,1024]{2,1,0:T(8,128)(2,1)}) custom-call(bf16[1024,1024]{1,0:T(8,128)(2,1)} %get-tuple-element.101.shared_ref.refs_0_.refs_14_, bf16[4,1024,1024]{2,1,0:T(8,128)(2,1)} %refs_2_.1, ...), custom_call_target="tpu_custom_call", output_to_operand_aliasing={{0}: (3, {}), {1}: (4, {}), {2}: (5, {})} | custom-call | flops 4294967296 | bytes 16777216 | tf_op jit(solution)/shard_map/forward/pallas_call | solution.py:115
  68.6 4.1 %collective-permute-done.12.refs_3_ = bf16[2,1,128,1024]{3,2,1,0:T(8,128)(2,1)S(1)} collective-permute-done((bf16[2,1,128,1024]{3,2,1,0:T(8,128)(2,1)S(1)}, bf16[2,1,128,1024]{3,2,1,0:T(8,128)(2,1)S(1)}, u32[]{:S(2)}, u32[]{:S(2)}) %collective-permute-start.12) | collective-permute-done | bytes 524320 | tf_op jit(solution)/shard_map/ppermute | solution.py:540
  74.8 8.6 %forward.5 = (bf16[4,1024,1024]{2,1,0:T(8,128)(2,1)}, bf16[4,1024,1024]{2,1,0:T(8,128)(2,1)}, bf16[4,1024,1024]{2,1,0:T(8,128)(2,1)}) custom-call(bf16[1024,1024]{1,0:T(8,128)(2,1)} %get-tuple-element.101.shared_ref.refs_0_.refs_14_, bf16[4,1024,1024]{2,1,0:T(8,128)(2,1)} %refs_2_.1, ...), custom_call_target="tpu_custom_call", output_to_operand_aliasing={{0}: (3, {}), {1}: (4, {}), {2}: (5, {})} | custom-call | flops 4294967296 | bytes 16777216 | tf_op jit(solution)/shard_map/forward/pallas_call | solution.py:115
  83.4 4.3 %collective-permute-done.13.refs_6_ = bf16[2,2,128,1024]{3,2,1,0:T(8,128)(2,1)} collective-permute-done((bf16[2,2,128,1024]{3,2,1,0:T(8,128)(2,1)S(1)}, bf16[2,2,128,1024]{3,2,1,0:T(8,128)(2,1)}, u32[]{:S(2)}, u32[]{:S(2)}) %collective-permute-start.13) | collective-permute-done | bytes 1048608 | tf_op jit(solution)/shard_map/ppermute | solution.py:540
  87.7 9.9 %mix.1 = (bf16[4,512,1024]{2,1,0:T(8,128)(2,1)}, bf16[4,512,1024]{2,1,0:T(8,128)(2,1)}) custom-call(s32[65]{0:T(128)} %stack.49.ids_ref, f32[1024,64]{1,0:T(8,128)} %get-tuple-element.106.gates_ref.refs_7_.refs_4_, bf16[4,1024,1024]{2,1,0:T(8,128)(2,1)} %get-tuple-element.107.outs_ref.refs_8_), custom_call_target="tpu_custom_call" | custom-call | flops 2147483648 | bytes 16777216 | tf_op jit(solution)/shard_map/mix/pallas_call | solution.py:191
  98.7 10.4 %spread_grads.2 = (bf16[4,1024,1024]{2,1,0:T(8,128)(2,1)}, f32[1024,64]{1,0:T(8,128)}) custom-call(s32[65]{0:T(128)} %stack.49.ids_ref, bf16[4,128,1024]{2,1,0:T(8,128)(2,1)} %bitcast.97, bf16[1,1,128,1024]{3,2,1,0:T(8,128)(2,1)} %bitcast.107, bf16[1,1,128,1024]{3,2,1,0:T(8,128)(2,1)} %bitcast.117, bf16[2,1,128,1024]{3,2,1,0:T(8,128)(2,1)} %copy-done.16, ...), custom_call_target="tpu_custom_call" | custom-call | flops 1073741824 | bytes 16777216 | tf_op jit(solution)/shard_map/spread_grads/pallas_call | solution.py:286
  113.1 10.2 %spread_grads.3 = (bf16[4,1024,1024]{2,1,0:T(8,128)(2,1)}, f32[1024,64]{1,0:T(8,128)}) custom-call(s32[65]{0:T(128)} %stack.49.ids_ref, bf16[4,128,1024]{2,1,0:T(8,128)(2,1)} %copy-done.13, bf16[1,1,128,1024]{3,2,1,0:T(8,128)(2,1)} %bitcast.124, bf16[1,1,128,1024]{3,2,1,0:T(8,128)(2,1)} %bitcast.125, ...), custom_call_target="tpu_custom_call", output_to_operand_aliasing={{0}: (10, {}), {1}: (11, {})} | custom-call | flops 1073741824 | bytes 16777216 | tf_op jit(solution)/shard_map/spread_grads/pallas_call | solution.py:286
  123.3 28.5 %backward.1 = (bf16[4,1024,1024]{2,1,0:T(8,128)(2,1)}, bf16[4,128,1152]{2,1,0:T(8,128)(2,1)}, bf16[4,128,1152]{2,1,0:T(8,128)(2,1)}) custom-call(s32[65]{0:T(128)} %stack.49.ids_ref, bf16[4,1024,1024]{2,1,0:T(8,128)(2,1)} %get-tuple-element.123.refs_0_.refs_2_, bf16[4,1024,1024]{2,1,0:T(8,128)(2,1)} %get-tuple-element.124.refs_1_, ...), custom_call_target="tpu_custom_call" | custom-call | flops 17179869184 | bytes 16777216 | tf_op jit(solution)/shard_map/backward/pallas_call | solution.py:389
  157.6 13.6 %weight_grads.3 = (bf16[4,1024,1024]{2,1,0:T(8,128)(2,1)}, bf16[4,1024,1024]{2,1,0:T(8,128)(2,1)}) custom-call(bf16[1024,1024]{1,0:T(8,128)(2,1)} %get-tuple-element.101.shared_ref.refs_0_.refs_14_, bf16[4,1024,1024]{2,1,0:T(8,128)(2,1)} %get-tuple-element.141.refs_1_, bf16[4,1024,1024]{2,1,0:T(8,128)(2,1)} %get-tuple-element.123.refs_0_.refs_2_, ...), custom_call_target="tpu_custom_call" | custom-call | flops 8589934592 | bytes 16777216 | tf_op jit(solution)/shard_map/weight_grads/pallas_call | solution.py:427
  171.2 5.4 %collective-permute-done.24 = bf16[512,1024]{1,0:T(8,128)(2,1)} collective-permute-done((bf16[512,1024]{1,0:T(8,128)(2,1)}, bf16[512,1024]{1,0:T(8,128)(2,1)}, u32[]{:S(2)}, u32[]{:S(2)}) %collective-permute-start.24) | collective-permute-done | bytes 1048608 | tf_op jit(solution)/shard_map/ppermute | solution.py:540
  182.2 8.6 %weight_grads.4 = (bf16[4,1024,1024]{2,1,0:T(8,128)(2,1)}, bf16[4,1024,1024]{2,1,0:T(8,128)(2,1)}) custom-call(bf16[1024,1024]{1,0:T(8,128)(2,1)} %get-tuple-element.101.shared_ref.refs_0_.refs_14_, bf16[4,1024,1024]{2,1,0:T(8,128)(2,1)} %get-tuple-element.141.refs_1_, ...), custom_call_target="tpu_custom_call", output_to_operand_aliasing={{0}: (4, {}), {1}: (5, {})} | custom-call | flops 4294967296 | bytes 16777216 | tf_op jit(solution)/shard_map/weight_grads/pallas_call | solution.py:427
  196.9 8.6 %weight_grads.5 = (bf16[4,1024,1024]{2,1,0:T(8,128)(2,1)}, bf16[4,1024,1024]{2,1,0:T(8,128)(2,1)}) custom-call(bf16[1024,1024]{1,0:T(8,128)(2,1)} %get-tuple-element.101.shared_ref.refs_0_.refs_14_, bf16[4,1024,1024]{2,1,0:T(8,128)(2,1)} %get-tuple-element.141.refs_1_, ...), custom_call_target="tpu_custom_call", output_to_operand_aliasing={{0}: (4, {}), {1}: (5, {})} | custom-call | flops 4294967296 | bytes 16777216 | tf_op jit(solution)/shard_map/weight_grads/pallas_call | solution.py:427
  205.6 3.5 %collective-permute-done.27 = bf16[4,32,1152]{2,1,0:T(8,128)(2,1)S(1)} collective-permute-done((bf16[4,32,1152]{2,1,0:T(8,128)(2,1)S(1)}, bf16[4,32,1152]{2,1,0:T(8,128)(2,1)S(1)}, u32[]{:S(2)}, u32[]{:S(2)}) %collective-permute-start.27) | collective-permute-done | bytes 294944 | tf_op jit(solution)/shard_map/ppermute | solution.py:540
  217.5 3.7 %collective-permute-done.31 = bf16[4,32,1152]{2,1,0:T(8,128)(2,1)S(1)} collective-permute-done((bf16[4,32,1152]{2,1,0:T(8,128)(2,1)S(1)}, bf16[4,32,1152]{2,1,0:T(8,128)(2,1)S(1)}, u32[]{:S(2)}, u32[]{:S(2)}) %collective-permute-start.31) | collective-permute-done | bytes 294944 | tf_op jit(solution)/shard_map/ppermute | solution.py:540
  223.4 5.1 %collective-permute-done.32 = bf16[4,32,1152]{2,1,0:T(8,128)(2,1)S(1)} collective-permute-done((bf16[4,32,1152]{2,1,0:T(8,128)(2,1)S(1)}, bf16[4,32,1152]{2,1,0:T(8,128)(2,1)S(1)}, u32[]{:S(2)}, u32[]{:S(2)}) %collective-permute-start.32) | collective-permute-done | bytes 294944 | tf_op jit(solution)/shard_map/ppermute | solution.py:540
  232.4 6.3 %collective-permute-done.33.refs_2_.refs_8_ = bf16[2,4,32,1152]{3,2,1,0:T(8,128)(2,1)S(1)} collective-permute-done((bf16[2,4,32,1152]{3,2,1,0:T(8,128)(2,1)S(1)}, bf16[2,4,32,1152]{3,2,1,0:T(8,128)(2,1)S(1)}, u32[]{:S(2)}, u32[]{:S(2)}) %collective-permute-start.33) | collective-permute-done | bytes 589856 | tf_op jit(solution)/shard_map/ppermute | solution.py:540
  242.0 7.2 %rows_grads.1 = (f32[1024,1024]{1,0:T(8,128)}, f32[1,1024]{1,0:T(1,128)}, f32[64,1024]{1,0:T(8,128)}, f32[1,64]{1,0:T(1,128)}) custom-call(s32[65]{0:T(128)} %stack.49.ids_ref, bf16[1,4,32,1152]{3,2,1,0:T(8,128)(2,1)} %bitcast.94, bf16[1,4,32,1152]{3,2,1,0:T(8,128)(2,1)} %bitcast.101, bf16[2,4,32,1152]{3,2,1,0:T(8,128)(2,1)} %copy-done.5, ...), custom_call_target="tpu_custom_call" | custom-call | flops 2147483648 | bytes 16777216 | tf_op jit(solution)/shard_map/rows_grads/pallas_call | solution.py:484
  (155 shorter events, 55.9 us)
Async XLA Ops:
  0.6 12.6 %collective-permute-start = (bf16[128,1024]{1,0:T(8,128)(2,1)}, bf16[128,1024]{1,0:T(8,128)(2,1)S(1)}, u32[]{:S(2)}, u32[]{:S(2)}) collective-permute-start(bf16[128,1024]{1,0:T(8,128)(2,1)} %refs_0_.1), channel_id=1, source_target_pairs={{0,24},{1,25},{2,26},{3,27},{4,28},{5,29},{6,30},{7,31},{8,16},{9,... | collective-permute-start | bytes 786440 | tf_op jit(solution)/shard_map/ppermute | solution.py:540
  5.7 12.2 %collective-permute-start.1 = (bf16[128,1024]{1,0:T(8,128)(2,1)}, bf16[128,1024]{1,0:T(8,128)(2,1)S(1)}, u32[]{:S(2)}, u32[]{:S(2)}) collective-permute-start(bf16[128,1024]{1,0:T(8,128)(2,1)} %refs_0_.1), channel_id=1, source_target_pairs={{0,8},{1,9},{2,10},{3,11},{4,12},{5,13},{6,14},{7,15},{8,0},{9,1},... | collective-permute-start | bytes 786440 | tf_op jit(solution)/shard_map/ppermute | solution.py:540
  18.0 16.8 %collective-permute-start.7 = (bf16[4,128,1024]{2,1,0:T(8,128)(2,1)S(1)}, bf16[4,128,1024]{2,1,0:T(8,128)(2,1)S(1)}, u32[]{:S(2)}, u32[]{:S(2)}) collective-permute-start(bf16[4,128,1024]{2,1,0:T(8,128)(2,1)S(1)} %bitcast.96), channel_id=1, source_target_pairs={{0,4},{1,5},{2,6},{3,7},{4,0},{5,1},{6,2},{7,3},{8,12},{9,13},{10,... | collective-permute-start | bytes 3145736 | tf_op jit(solution)/shard_map/ppermute | solution.py:540
  19.0 11.3 %collective-permute-start.6 = (bf16[128,1024]{1,0:T(8,128)(2,1)S(1)}, bf16[128,1024]{1,0:T(8,128)(2,1)S(1)}, u32[]{:S(2)}, u32[]{:S(2)}) collective-permute-start(bf16[128,1024]{1,0:T(8,128)(2,1)S(1)} %dynamic-slice_bitcast_fusion.4), channel_id=1, source_target_pairs={{0,24},{1,25},{2,26},{3,27},{4,28},{5,29},{6,30},{7,31},{8,16},{9,... | collective-permute-start | bytes 786440 | tf_op jit(solution)/shard_map/ppermute | solution.py:540
  21.3 13.5 %collective-permute-start.2 = (bf16[128,1024]{1,0:T(8,128)(2,1)S(1)}, bf16[128,1024]{1,0:T(8,128)(2,1)S(1)}, u32[]{:S(2)}, u32[]{:S(2)}) collective-permute-start(bf16[128,1024]{1,0:T(8,128)(2,1)S(1)} %collective-permute-done.refs_1_), channel_id=1, source_target_pairs={{0,8},{1,9},{2,10},{3,11},{4,12},{5,13},{6,14},{7,15},{8,0},{9,1},... | collective-permute-start | bytes 786440 | tf_op jit(solution)/shard_map/ppermute | solution.py:540
  41.3 16.5 %collective-permute-start.9 = (bf16[2,128,1024]{2,1,0:T(8,128)(2,1)S(1)}, bf16[2,128,1024]{2,1,0:T(8,128)(2,1)S(1)}, u32[]{:S(2)}, u32[]{:S(2)}) collective-permute-start(bf16[2,128,1024]{2,1,0:T(8,128)(2,1)S(1)} %pad_maximum_fusion.4), channel_id=1, source_target_pairs={{0,8},{1,9},{2,10},{3,11},{4,12},{5,13},{6,14},{7,15},{8,0},{9,1},... | collective-permute-start | bytes 1572872 | tf_op jit(solution)/shard_map/ppermute | solution.py:540
  41.4 16.4 %collective-permute-start.10 = (bf16[1,128,1024]{2,1,0:T(8,128)(2,1)S(1)}, bf16[1,128,1024]{2,1,0:T(8,128)(2,1)S(1)}, u32[]{:S(2)}, u32[]{:S(2)}) collective-permute-start(bf16[1,128,1024]{2,1,0:T(8,128)(2,1)S(1)} %bitcast.104), channel_id=1, source_target_pairs={{0,1},{1,0},{2,3},{3,2},{4,6},{5,7},{6,4},{7,5},{8,9},{9,8},{10,11... | collective-permute-start | bytes 786440 | tf_op jit(solution)/shard_map/ppermute | solution.py:540
  57.9 14.7 %collective-permute-start.12 = (bf16[2,1,128,1024]{3,2,1,0:T(8,128)(2,1)S(1)}, bf16[2,1,128,1024]{3,2,1,0:T(8,128)(2,1)S(1)}, u32[]{:S(2)}, u32[]{:S(2)}) collective-permute-start(bf16[2,1,128,1024]{3,2,1,0:T(8,128)(2,1)S(1)} %pad_maximum_fusion.5), channel_id=1, source_target_pairs={{0,2},{1,3},{2,0},{3,1},{4,5},{5,4},{6,7},{7,6},{8,10},{9,11},{10,... | collective-permute-start | bytes 1572872 | tf_op jit(solution)/shard_map/ppermute | solution.py:540
  59.5 13.2 %collective-permute-start.11 = (bf16[2,128,1024]{2,1,0:T(8,128)(2,1)S(1)}, bf16[2,128,1024]{2,1,0:T(8,128)(2,1)S(1)}, u32[]{:S(2)}, u32[]{:S(2)}) collective-permute-start(bf16[2,128,1024]{2,1,0:T(8,128)(2,1)S(1)} %collective-permute-done.9), channel_id=1, source_target_pairs={{0,1},{1,0},{2,3},{3,2},{4,6},{5,7},{6,4},{7,5},{8,9},{9,8},{10,11... | collective-permute-start | bytes 1572872 | tf_op jit(solution)/shard_map/ppermute | solution.py:540
  72.7 15.0 %collective-permute-start.13 = (bf16[2,2,128,1024]{3,2,1,0:T(8,128)(2,1)S(1)}, bf16[2,2,128,1024]{3,2,1,0:T(8,128)(2,1)}, u32[]{:S(2)}, u32[]{:S(2)}) collective-permute-start(bf16[2,2,128,1024]{3,2,1,0:T(8,128)(2,1)S(1)} %pad_maximum_fusion), channel_id=1, source_target_pairs={{0,2},{1,3},{2,0},{3,1},{4,5},{5,4},{6,7},{7,6},{8,10},{9,11},{10,... | collective-permute-start | bytes 3145736 | tf_op jit(solution)/shard_map/ppermute | solution.py:540
  97.6 11.5 %collective-permute-start.17 = (bf16[4,512,1024]{2,1,0:T(8,128)(2,1)}, bf16[4,512,1024]{2,1,0:T(8,128)(2,1)}, u32[]{:S(2)}, u32[]{:S(2)}) collective-permute-start(bf16[4,512,1024]{2,1,0:T(8,128)(2,1)} %get-tuple-element.109), channel_id=1, source_target_pairs={{0,4},{1,5},{2,6},{3,7},{4,0},{5,1},{6,2},{7,3},{8,12},{9,13},{10,... | collective-permute-start | bytes 12582920 | tf_op jit(solution)/shard_map/ppermute | solution.py:540
  97.7 14.6 %collective-permute-start.21 = (bf16[2,2,128,1024]{3,2,1,0:T(8,128)(2,1)}, bf16[2,2,128,1024]{3,2,1,0:T(8,128)(2,1)}, u32[]{:S(2)}, u32[]{:S(2)}) collective-permute-start(bf16[2,2,128,1024]{3,2,1,0:T(8,128)(2,1)} %collective-permute-done.13.refs_6_), channel_id=1, source_target_pairs={{0,4},{1,5},{2,6},{3,7},{4,0},{5,1},{6,2},{7,3},{8,12},{9,13},{10,... | collective-permute-start | bytes 3145736 | tf_op jit(solution)/shard_map/ppermute | solution.py:540
  98.2 14.1 %collective-permute-start.19 = (bf16[2,128,1024]{2,1,0:T(8,128)(2,1)S(1)}, bf16[2,128,1024]{2,1,0:T(8,128)(2,1)S(1)}, u32[]{:S(2)}, u32[]{:S(2)}) collective-permute-start(bf16[2,128,1024]{2,1,0:T(8,128)(2,1)S(1)} %collective-permute-done.9), channel_id=1, source_target_pairs={{0,4},{1,5},{2,6},{3,7},{4,0},{5,1},{6,2},{7,3},{8,12},{9,13},{10,... | collective-permute-start | bytes 1572872 | tf_op jit(solution)/shard_map/ppermute | solution.py:540
  98.3 14.0 %collective-permute-start.20 = (bf16[2,128,1024]{2,1,0:T(8,128)(2,1)S(1)}, bf16[2,128,1024]{2,1,0:T(8,128)(2,1)}, u32[]{:S(2)}, u32[]{:S(2)}) collective-permute-start(bf16[2,128,1024]{2,1,0:T(8,128)(2,1)S(1)} %collective-permute-done.11), channel_id=1, source_target_pairs={{0,4},{1,5},{2,6},{3,7},{4,0},{5,1},{6,2},{7,3},{8,12},{9,13},{10,... | collective-permute-start | bytes 1572872 | tf_op jit(solution)/shard_map/ppermute | solution.py:540
  111.7 40.2 %collective-permute-start.18 = (bf16[2,512,1024]{2,1,0:T(8,128)(2,1)S(1)}, bf16[2,512,1024]{2,1,0:T(8,128)(2,1)}, u32[]{:S(2)}, u32[]{:S(2)}) collective-permute-start(bf16[2,512,1024]{2,1,0:T(8,128)(2,1)S(1)} %add_convert_fusion), channel_id=1, source_target_pairs={{0,1},{1,0},{2,3},{3,2},{4,6},{5,7},{6,4},{7,5},{8,9},{9,8},{10,11... | collective-permute-start | bytes 6291464 | tf_op jit(solution)/shard_map/ppermute | solution.py:540
  155.2 21.4 %collective-permute-start.24 = (bf16[512,1024]{1,0:T(8,128)(2,1)}, bf16[512,1024]{1,0:T(8,128)(2,1)}, u32[]{:S(2)}, u32[]{:S(2)}) collective-permute-start(bf16[512,1024]{1,0:T(8,128)(2,1)} %fusion.4), channel_id=1, source_target_pairs={{0,2},{1,3},{2,0},{3,1},{4,5},{5,4},{6,7},{7,6},{8,10},{9,11},{10,... | collective-permute-start | bytes 3145736 | tf_op jit(solution)/shard_map/ppermute | solution.py:540
  156.4 20.2 %collective-permute-start.23 = (bf16[2,128,1152]{2,1,0:T(8,128)(2,1)S(1)}, bf16[2,128,1152]{2,1,0:T(8,128)(2,1)S(1)}, u32[]{:S(2)}, u32[]{:S(2)}) collective-permute-start(bf16[2,128,1152]{2,1,0:T(8,128)(2,1)S(1)} %add_convert_fusion.2), channel_id=1, source_target_pairs={{0,1},{1,0},{2,3},{3,2},{4,6},{5,7},{6,4},{7,5},{8,9},{9,8},{10,11... | collective-permute-start | bytes 1769480 | tf_op jit(solution)/shard_map/ppermute | solution.py:540
  178.3 13.7 %collective-permute-start.26 = (bf16[256,1024]{1,0:T(8,128)(2,1)S(1)}, bf16[256,1024]{1,0:T(8,128)(2,1)}, u32[]{:S(2)}, u32[]{:S(2)}) collective-permute-start(bf16[256,1024]{1,0:T(8,128)(2,1)S(1)} %fusion.5), channel_id=1, source_target_pairs={{0,8},{1,9},{2,10},{3,11},{4,12},{5,13},{6,14},{7,15},{8,0},{9,1},... | collective-permute-start | bytes 1572872 | tf_op jit(solution)/shard_map/ppermute | solution.py:540
  194.1 11.4 %collective-permute-start.28 = (bf16[128,1024]{1,0:T(8,128)(2,1)}, bf16[128,1024]{1,0:T(8,128)(2,1)S(1)}, u32[]{:S(2)}, u32[]{:S(2)}) collective-permute-start(bf16[128,1024]{1,0:T(8,128)(2,1)} %fusion.9), channel_id=1, source_target_pairs={{0,24},{1,25},{2,26},{3,27},{4,28},{5,29},{6,30},{7,31},{8,16},{9,... | collective-permute-start | bytes 786440 | tf_op jit(solution)/shard_map/ppermute | solution.py:540
  196.1 13.0 %collective-permute-start.27 = (bf16[4,32,1152]{2,1,0:T(8,128)(2,1)S(1)}, bf16[4,32,1152]{2,1,0:T(8,128)(2,1)S(1)}, u32[]{:S(2)}, u32[]{:S(2)}) collective-permute-start(bf16[4,32,1152]{2,1,0:T(8,128)(2,1)S(1)} %bitcast.114), channel_id=1, source_target_pairs={{0,8},{1,9},{2,10},{3,11},{4,12},{5,13},{6,14},{7,15},{8,0},{9,1},... | collective-permute-start | bytes 884744 | tf_op jit(solution)/shard_map/ppermute | solution.py:540
  217.0 13.3 %collective-permute-start.30 = (bf16[2,128,1024]{2,1,0:T(8,128)(2,1)S(1)}, bf16[2,128,1024]{2,1,0:T(8,128)(2,1)S(1)}, u32[]{:S(2)}, u32[]{:S(2)}) collective-permute-start(bf16[2,128,1024]{2,1,0:T(8,128)(2,1)S(1)} %pad_maximum_fusion.6), channel_id=1, source_target_pairs={{0,2},{1,3},{2,0},{3,1},{4,5},{5,4},{6,7},{7,6},{8,10},{9,11},{10,... | collective-permute-start | bytes 1572872 | tf_op jit(solution)/shard_map/ppermute | solution.py:540
  223.4 17.6 %collective-permute-start.34 = (bf16[1,4,32,1152]{3,2,1,0:T(8,128)(2,1)S(1)}, bf16[1,4,32,1152]{3,2,1,0:T(8,128)(2,1)S(1)}, u32[]{:S(2)}, u32[]{:S(2)}) collective-permute-start(bf16[1,4,32,1152]{3,2,1,0:T(8,128)(2,1)S(1)} %bitcast.91), channel_id=1, source_target_pairs={{0,4},{1,5},{2,6},{3,7},{4,0},{5,1},{6,2},{7,3},{8,12},{9,13},{10,... | collective-permute-start | bytes 884744 | tf_op jit(solution)/shard_map/ppermute | solution.py:540
  228.6 12.5 %collective-permute-start.35 = (bf16[1,4,32,1152]{3,2,1,0:T(8,128)(2,1)S(1)}, bf16[1,4,32,1152]{3,2,1,0:T(8,128)(2,1)S(1)}, u32[]{:S(2)}, u32[]{:S(2)}) collective-permute-start(bf16[1,4,32,1152]{3,2,1,0:T(8,128)(2,1)S(1)} %bitcast.99), channel_id=1, source_target_pairs={{0,4},{1,5},{2,6},{3,7},{4,0},{5,1},{6,2},{7,3},{8,12},{9,13},{10,... | collective-permute-start | bytes 884744 | tf_op jit(solution)/shard_map/ppermute | solution.py:540
  228.9 9.9 %collective-permute-start.33 = (bf16[2,4,32,1152]{3,2,1,0:T(8,128)(2,1)S(1)}, bf16[2,4,32,1152]{3,2,1,0:T(8,128)(2,1)S(1)}, u32[]{:S(2)}, u32[]{:S(2)}) collective-permute-start(bf16[2,4,32,1152]{3,2,1,0:T(8,128)(2,1)S(1)} %pad_maximum_fusion.3), channel_id=1, source_target_pairs={{0,2},{1,3},{2,0},{3,1},{4,5},{5,4},{6,7},{7,6},{8,10},{9,11},{10,... | collective-permute-start | bytes 1769480 | tf_op jit(solution)/shard_map/ppermute | solution.py:540
  (42 other events, 384.7 us)
where the time goes:
time: 252 us; the launch traced here: 249 us
  Pallas kernels  140 us (56%)
  waiting for transfers between devices  52.8 us (21%)
  starting transfers between devices  32.7 us (13%)
  other arithmetic  13 us (5%)
  local copies, waits for them, and re-layouts  7.6 us (3%)
    ppermute x37, waiting for transfers between devices, move(): return lax.ppermute(x, ('dp', 'expert'), pairs)  52.8 us
    ppermute x37, starting transfers between devices, move(): return lax.ppermute(x, ('dp', 'expert'), pairs)  32.7 us
    pallas_call x3, Pallas kernels, forward(): pl.pallas_call(forward_kernel, grid=(count, rows // sub), in_specs=[pl.Bl...  31.9 us
    pallas_call x3, Pallas kernels, weight_grads(): pl.pallas_call(functools.partial(weights_kernel, n), grid=(count, 2), in_...  30.8 us
    pallas_call x1, Pallas kernels, backward(): pl.pallas_call(functools.partial(backward_kernel, tasks, cols // tasks, n...  28.5 us
    pallas_call x2, Pallas kernels, spread_grads(): pl.pallas_call(functools.partial(spread_kernel, tasks, cols // tasks, pla...  20.6 us
    pallas_call x2, Pallas kernels, cross(): pl.pallas_call(functools.partial(cross_kernel, cols // tasks, n), grid=(2...  10.8 us
    pallas_call x1, Pallas kernels, mix(): pl.pallas_call(functools.partial(mix_kernel, tasks, cols // tasks, rows /...  9.89 us
  transfers between devices with their start and end apart: 37, of which 14 were waited for; matrix products, arithmetic and copies ran while one was open for 6% of the time, Pallas kernels for 48%

commit v1 on v0

--- a/solution.py
+++ b/solution.py
@@ -388,7 +388,7 @@
         args, in_specs = args + [before[0]], in_specs + [pl.BlockSpec(memory_space=pl.ANY)]
     return pl.pallas_call(
         functools.partial(
-            backward_kernel, tasks, cols // tasks, n, min(rows, 512), start, last
+            backward_kernel, tasks, cols // tasks, n, min(rows, 1024), start, last
         ),
         grid_spec=pltpu.PrefetchScalarGridSpec(
             num_scalar_prefetch=1,
@@ -663,10 +663,12 @@
 
 def finish(steps, *after):
     moved = tie([s.moved or () for s in steps], *after)
+    earlier = None
     for one, arrays in zip(steps, moved):
         if one.moved is not None:
             one.moved = arrays
-            one.finish()
+            one.finish(earlier)
+            earlier = one.operand
 
 
 def tie(x, *others):
@@ -813,7 +815,11 @@
         mixed.start()
         tied = [tie(a, *ready) for a in acts]
         weights = weight_grads(shared, tied, ogs, pgs, b, size, weights)
-        finish([total, mixed], weights[0])
+        if b + size < local:
+            finish([total, mixed], weights[0])
+        else:
+            total.finish(weights[0])
+            mixed.finish(weights[0], total.operand)
     up_grad, down_grad = weights
     total = total.result()
     task_mixed = mixed.result().astype(BF16)

time: 252 us -> 248 us (0.984)
  no operation moved by 1% of the time
where the time goes in v1:
time: 248 us; the launch traced here: 247 us
  Pallas kernels  139 us (56%)
  waiting for transfers between devices  53.6 us (22%)
  starting transfers between devices  30.9 us (12%)
  other arithmetic  12.3 us (5%)
  local copies, waits for them, and re-layouts  7.61 us (3%)
    ppermute x37, waiting for transfers between devices, move(): return lax.ppermute(x, ('dp', 'expert'), pairs)  53.6 us
    pallas_call x3, Pallas kernels, forward(): pl.pallas_call(forward_kernel, grid=(count, rows // sub), in_specs=[pl.Bl...  31.9 us
    ppermute x37, starting transfers between devices, move(): return lax.ppermute(x, ('dp', 'expert'), pairs)  30.9 us
    pallas_call x3, Pallas kernels, weight_grads(): pl.pallas_call(functools.partial(weights_kernel, n), grid=(count, 2), in_...  30.8 us
    pallas_call x1, Pallas kernels, backward(): pl.pallas_call(functools.partial(backward_kernel, tasks, cols // tasks, n...  27.7 us
    pallas_call x2, Pallas kernels, spread_grads(): pl.pallas_call(functools.partial(spread_kernel, tasks, cols // tasks, pla...  20.6 us
    pallas_call x2, Pallas kernels, cross(): pl.pallas_call(functools.partial(cross_kernel, cols // tasks, n), grid=(2...  10.8 us
    pallas_call x1, Pallas kernels, mix(): pl.pallas_call(functools.partial(mix_kernel, tasks, cols // tasks, rows /...  9.89 us
  transfers between devices with their start and end apart: 37, of which 14 were waited for; matrix products, arithmetic and copies ran while one was open for 6% of the time, Pallas kernels for 48%

profile of v1, /device:TPU:0, one launch (start us, length us, event | category | flops | bytes accessed | tf_op | source)
XLA Modules:
  0.0 247.0 jit_solution(695417633619217256)
XLA Ops:
  0.6 5.1 %collective-permute-start = (bf16[128,1024]{1,0:T(8,128)(2,1)}, bf16[128,1024]{1,0:T(8,128)(2,1)S(1)}, u32[]{:S(2)}, u32[]{:S(2)}) collective-permute-start(bf16[128,1024]{1,0:T(8,128)(2,1)} %refs_0_.1), channel_id=1, source_target_pairs={{0,24},{1,25},{2,26},{3,27},{4,28},{5,29},{6,30},{7,31},{8,16},{9,... | collective-permute-start | bytes 786440 | tf_op jit(solution)/shard_map/ppermute | solution.py:540
  7.3 5.9 %collective-permute-done.refs_1_ = bf16[128,1024]{1,0:T(8,128)(2,1)S(1)} collective-permute-done((bf16[128,1024]{1,0:T(8,128)(2,1)}, bf16[128,1024]{1,0:T(8,128)(2,1)S(1)}, u32[]{:S(2)}, u32[]{:S(2)}) %collective-permute-start) | collective-permute-done | bytes 262176 | tf_op jit(solution)/shard_map/ppermute | solution.py:540
  13.2 4.8 %collective-permute-done.1.refs_2_ = bf16[128,1024]{1,0:T(8,128)(2,1)S(1)} collective-permute-done((bf16[128,1024]{1,0:T(8,128)(2,1)}, bf16[128,1024]{1,0:T(8,128)(2,1)S(1)}, u32[]{:S(2)}, u32[]{:S(2)}) %collective-permute-start.1) | collective-permute-done | bytes 262176 | tf_op jit(solution)/shard_map/ppermute | solution.py:540
  23.7 6.6 %cross.2 = (bf16[1024,1024]{1,0:T(8,128)(2,1)}, bf16[1024,1024]{1,0:T(8,128)(2,1)}, f32[1024,64]{1,0:T(8,128)}) custom-call(bf16[128,1024]{1,0:T(8,128)(2,1)} %refs_0_.1, bf16[128,1024]{1,0:T(8,128)(2,1)} %copy-done.24, bf16[128,1024]{1,0:T(8,128)(2,1)} %copy-done.25, bf16[128,1024]{1,0:T(8,128)(2,1)} %copy-done.26, bf16[128,1024]{1,0:T(8,128)(2,1)} %copy-done.27, ...), custom_call_target="tpu_custom_call" | custom-call | flops 1610612736 | bytes 16777216 | tf_op jit(solution)/shard_map/cross/pallas_call | solution.py:78
  30.4 4.4 %collective-permute-done.2.refs_0_ = bf16[128,1024]{1,0:T(8,128)(2,1)S(1)} collective-permute-done((bf16[128,1024]{1,0:T(8,128)(2,1)S(1)}, bf16[128,1024]{1,0:T(8,128)(2,1)S(1)}, u32[]{:S(2)}, u32[]{:S(2)}) %collective-permute-start.2) | collective-permute-done | bytes 262176 | tf_op jit(solution)/shard_map/ppermute | solution.py:540
  37.1 4.2 %cross.3 = (bf16[1024,1024]{1,0:T(8,128)(2,1)}, bf16[1024,1024]{1,0:T(8,128)(2,1)}, f32[1024,64]{1,0:T(8,128)}) custom-call(bf16[128,1024]{1,0:T(8,128)(2,1)} %copy-done.20, bf16[128,1024]{1,0:T(8,128)(2,1)} %copy-done.21, bf16[1024,1024]{1,0:T(8,128)(2,1)} %bitcast.90, ...), custom_call_target="tpu_custom_call", output_to_operand_aliasing={{0}: (6, {}), {1}: (7, {}), {2}: (8, {})} | custom-call | flops 536870912 | bytes 16777216 | tf_op jit(solution)/shard_map/cross/pallas_call | solution.py:78
  43.0 14.8 %forward.3 = (bf16[4,1024,1024]{2,1,0:T(8,128)(2,1)}, bf16[4,1024,1024]{2,1,0:T(8,128)(2,1)}, bf16[4,1024,1024]{2,1,0:T(8,128)(2,1)}) custom-call(bf16[1024,1024]{1,0:T(8,128)(2,1)} %get-tuple-element.103.shared_ref.refs_0_.refs_14_, bf16[4,1024,1024]{2,1,0:T(8,128)(2,1)} %refs_2_.1, bf16[4,1024,1024]{2,1,0:T(8,128)(2,1)} %refs_3_.3), custom_call_target="tpu_custom_call" | custom-call | flops 8589934592 | bytes 16777216 | tf_op jit(solution)/shard_map/forward/pallas_call | solution.py:115
  60.0 8.6 %forward.4 = (bf16[4,1024,1024]{2,1,0:T(8,128)(2,1)}, bf16[4,1024,1024]{2,1,0:T(8,128)(2,1)}, bf16[4,1024,1024]{2,1,0:T(8,128)(2,1)}) custom-call(bf16[1024,1024]{1,0:T(8,128)(2,1)} %get-tuple-element.103.shared_ref.refs_0_.refs_14_, bf16[4,1024,1024]{2,1,0:T(8,128)(2,1)} %refs_2_.1, ...), custom_call_target="tpu_custom_call", output_to_operand_aliasing={{0}: (3, {}), {1}: (4, {}), {2}: (5, {})} | custom-call | flops 4294967296 | bytes 16777216 | tf_op jit(solution)/shard_map/forward/pallas_call | solution.py:115
  68.6 4.1 %collective-permute-done.12.refs_3_ = bf16[2,1,128,1024]{3,2,1,0:T(8,128)(2,1)S(1)} collective-permute-done((bf16[2,1,128,1024]{3,2,1,0:T(8,128)(2,1)S(1)}, bf16[2,1,128,1024]{3,2,1,0:T(8,128)(2,1)S(1)}, u32[]{:S(2)}, u32[]{:S(2)}) %collective-permute-start.12) | collective-permute-done | bytes 524320 | tf_op jit(solution)/shard_map/ppermute | solution.py:540
  74.8 8.6 %forward.5 = (bf16[4,1024,1024]{2,1,0:T(8,128)(2,1)}, bf16[4,1024,1024]{2,1,0:T(8,128)(2,1)}, bf16[4,1024,1024]{2,1,0:T(8,128)(2,1)}) custom-call(bf16[1024,1024]{1,0:T(8,128)(2,1)} %get-tuple-element.103.shared_ref.refs_0_.refs_14_, bf16[4,1024,1024]{2,1,0:T(8,128)(2,1)} %refs_2_.1, ...), custom_call_target="tpu_custom_call", output_to_operand_aliasing={{0}: (3, {}), {1}: (4, {}), {2}: (5, {})} | custom-call | flops 4294967296 | bytes 16777216 | tf_op jit(solution)/shard_map/forward/pallas_call | solution.py:115
  83.4 4.3 %collective-permute-done.13.refs_6_ = bf16[2,2,128,1024]{3,2,1,0:T(8,128)(2,1)} collective-permute-done((bf16[2,2,128,1024]{3,2,1,0:T(8,128)(2,1)S(1)}, bf16[2,2,128,1024]{3,2,1,0:T(8,128)(2,1)}, u32[]{:S(2)}, u32[]{:S(2)}) %collective-permute-start.13) | collective-permute-done | bytes 1048608 | tf_op jit(solution)/shard_map/ppermute | solution.py:540
  87.7 9.9 %mix.1 = (bf16[4,512,1024]{2,1,0:T(8,128)(2,1)}, bf16[4,512,1024]{2,1,0:T(8,128)(2,1)}) custom-call(s32[65]{0:T(128)} %stack.49.ids_ref, f32[1024,64]{1,0:T(8,128)} %get-tuple-element.108.gates_ref.refs_7_.refs_4_, bf16[4,1024,1024]{2,1,0:T(8,128)(2,1)} %get-tuple-element.109.outs_ref.refs_8_), custom_call_target="tpu_custom_call" | custom-call | flops 2147483648 | bytes 16777216 | tf_op jit(solution)/shard_map/mix/pallas_call | solution.py:191
  98.7 10.4 %spread_grads.2 = (bf16[4,1024,1024]{2,1,0:T(8,128)(2,1)}, f32[1024,64]{1,0:T(8,128)}) custom-call(s32[65]{0:T(128)} %stack.49.ids_ref, bf16[4,128,1024]{2,1,0:T(8,128)(2,1)} %bitcast.97, bf16[1,1,128,1024]{3,2,1,0:T(8,128)(2,1)} %bitcast.107, bf16[1,1,128,1024]{3,2,1,0:T(8,128)(2,1)} %bitcast.117, bf16[2,1,128,1024]{3,2,1,0:T(8,128)(2,1)} %copy-done.16, ...), custom_call_target="tpu_custom_call" | custom-call | flops 1073741824 | bytes 16777216 | tf_op jit(solution)/shard_map/spread_grads/pallas_call | solution.py:286
  113.1 10.2 %spread_grads.3 = (bf16[4,1024,1024]{2,1,0:T(8,128)(2,1)}, f32[1024,64]{1,0:T(8,128)}) custom-call(s32[65]{0:T(128)} %stack.49.ids_ref, bf16[4,128,1024]{2,1,0:T(8,128)(2,1)} %copy-done.13, bf16[1,1,128,1024]{3,2,1,0:T(8,128)(2,1)} %bitcast.124, bf16[1,1,128,1024]{3,2,1,0:T(8,128)(2,1)} %bitcast.125, ...), custom_call_target="tpu_custom_call", output_to_operand_aliasing={{0}: (10, {}), {1}: (11, {})} | custom-call | flops 1073741824 | bytes 16777216 | tf_op jit(solution)/shard_map/spread_grads/pallas_call | solution.py:286
  123.3 27.7 %backward.1 = (bf16[4,1024,1024]{2,1,0:T(8,128)(2,1)}, bf16[4,128,1152]{2,1,0:T(8,128)(2,1)}, bf16[4,128,1152]{2,1,0:T(8,128)(2,1)}) custom-call(s32[65]{0:T(128)} %stack.49.ids_ref, bf16[4,1024,1024]{2,1,0:T(8,128)(2,1)} %get-tuple-element.125.refs_0_.refs_2_, bf16[4,1024,1024]{2,1,0:T(8,128)(2,1)} %get-tuple-element.126.refs_1_, ...), custom_call_target="tpu_custom_call" | custom-call | flops 17179869184 | bytes 16777216 | tf_op jit(solution)/shard_map/backward/pallas_call | solution.py:389
  151.1 3.2 %fusion.4 = bf16[512,1024]{1,0:T(8,128)(2,1)} fusion(bf16[2,512,1024]{2,1,0:T(8,128)(2,1)} %collective-permute-done.18, bf16[4,512,1024]{2,1,0:T(8,128)(2,1)} %collective-permute-done.17, bf16[4,512,1024]{2,1,0:T(8,128)(2,1)S(1)} %copy-done.3), kind=kLoop, calls=%fused_computation.10 | loop fusion | flops 3145728 | bytes 4194304 | tf_op jit(solution)/shard_map/convert_element_type | solution.py:606
  156.8 13.6 %weight_grads.3 = (bf16[4,1024,1024]{2,1,0:T(8,128)(2,1)}, bf16[4,1024,1024]{2,1,0:T(8,128)(2,1)}) custom-call(bf16[1024,1024]{1,0:T(8,128)(2,1)} %get-tuple-element.103.shared_ref.refs_0_.refs_14_, bf16[4,1024,1024]{2,1,0:T(8,128)(2,1)} %get-tuple-element.145.refs_1_, bf16[4,1024,1024]{2,1,0:T(8,128)(2,1)} %get-tuple-element.125.refs_0_.refs_2_, ...), custom_call_target="tpu_custom_call" | custom-call | flops 8589934592 | bytes 16777216 | tf_op jit(solution)/shard_map/weight_grads/pallas_call | solution.py:427
  170.4 5.4 %collective-permute-done.24 = bf16[512,1024]{1,0:T(8,128)(2,1)} collective-permute-done((bf16[512,1024]{1,0:T(8,128)(2,1)}, bf16[512,1024]{1,0:T(8,128)(2,1)}, u32[]{:S(2)}, u32[]{:S(2)}) %collective-permute-start.24) | collective-permute-done | bytes 1048608 | tf_op jit(solution)/shard_map/ppermute | solution.py:540
  181.4 8.6 %weight_grads.4 = (bf16[4,1024,1024]{2,1,0:T(8,128)(2,1)}, bf16[4,1024,1024]{2,1,0:T(8,128)(2,1)}) custom-call(bf16[1024,1024]{1,0:T(8,128)(2,1)} %get-tuple-element.103.shared_ref.refs_0_.refs_14_, bf16[4,1024,1024]{2,1,0:T(8,128)(2,1)} %get-tuple-element.145.refs_1_, ...), custom_call_target="tpu_custom_call", output_to_operand_aliasing={{0}: (4, {}), {1}: (5, {})} | custom-call | flops 4294967296 | bytes 16777216 | tf_op jit(solution)/shard_map/weight_grads/pallas_call | solution.py:427
  197.2 8.6 %weight_grads.5 = (bf16[4,1024,1024]{2,1,0:T(8,128)(2,1)}, bf16[4,1024,1024]{2,1,0:T(8,128)(2,1)}) custom-call(bf16[1024,1024]{1,0:T(8,128)(2,1)} %get-tuple-element.103.shared_ref.refs_0_.refs_14_, bf16[4,1024,1024]{2,1,0:T(8,128)(2,1)} %get-tuple-element.145.refs_1_, ...), custom_call_target="tpu_custom_call", output_to_operand_aliasing={{0}: (4, {}), {1}: (5, {})} | custom-call | flops 4294967296 | bytes 16777216 | tf_op jit(solution)/shard_map/weight_grads/pallas_call | solution.py:427
  215.9 3.1 %collective-permute-done.31 = bf16[4,32,1152]{2,1,0:T(8,128)(2,1)S(1)} collective-permute-done((bf16[4,32,1152]{2,1,0:T(8,128)(2,1)S(1)}, bf16[4,32,1152]{2,1,0:T(8,128)(2,1)S(1)}, u32[]{:S(2)}, u32[]{:S(2)}) %collective-permute-start.31) | collective-permute-done | bytes 294944 | tf_op jit(solution)/shard_map/ppermute | solution.py:540
  219.8 6.5 %collective-permute-done.32 = bf16[4,32,1152]{2,1,0:T(8,128)(2,1)S(1)} collective-permute-done((bf16[4,32,1152]{2,1,0:T(8,128)(2,1)S(1)}, bf16[4,32,1152]{2,1,0:T(8,128)(2,1)S(1)}, u32[]{:S(2)}, u32[]{:S(2)}) %collective-permute-start.32) | collective-permute-done | bytes 294944 | tf_op jit(solution)/shard_map/ppermute | solution.py:540
  229.0 7.4 %collective-permute-done.33.refs_2_.refs_8_ = bf16[2,4,32,1152]{3,2,1,0:T(8,128)(2,1)S(1)} collective-permute-done((bf16[2,4,32,1152]{3,2,1,0:T(8,128)(2,1)S(1)}, bf16[2,4,32,1152]{3,2,1,0:T(8,128)(2,1)S(1)}, u32[]{:S(2)}, u32[]{:S(2)}) %collective-permute-start.33) | collective-permute-done | bytes 589856 | tf_op jit(solution)/shard_map/ppermute | solution.py:540
  239.7 7.2 %rows_grads.1 = (f32[1024,1024]{1,0:T(8,128)}, f32[1,1024]{1,0:T(1,128)}, f32[64,1024]{1,0:T(8,128)}, f32[1,64]{1,0:T(1,128)}) custom-call(s32[65]{0:T(128)} %stack.49.ids_ref, bf16[1,4,32,1152]{3,2,1,0:T(8,128)(2,1)} %bitcast.94, bf16[1,4,32,1152]{3,2,1,0:T(8,128)(2,1)} %bitcast.101, bf16[2,4,32,1152]{3,2,1,0:T(8,128)(2,1)} %copy-done.5, ...), custom_call_target="tpu_custom_call" | custom-call | flops 2147483648 | bytes 16777216 | tf_op jit(solution)/shard_map/rows_grads/pallas_call | solution.py:484
  (155 shorter events, 52.6 us)
Async XLA Ops:
  0.6 12.6 %collective-permute-start = (bf16[128,1024]{1,0:T(8,128)(2,1)}, bf16[128,1024]{1,0:T(8,128)(2,1)S(1)}, u32[]{:S(2)}, u32[]{:S(2)}) collective-permute-start(bf16[128,1024]{1,0:T(8,128)(2,1)} %refs_0_.1), channel_id=1, source_target_pairs={{0,24},{1,25},{2,26},{3,27},{4,28},{5,29},{6,30},{7,31},{8,16},{9,... | collective-permute-start | bytes 786440 | tf_op jit(solution)/shard_map/ppermute | solution.py:540
  5.7 12.2 %collective-permute-start.1 = (bf16[128,1024]{1,0:T(8,128)(2,1)}, bf16[128,1024]{1,0:T(8,128)(2,1)S(1)}, u32[]{:S(2)}, u32[]{:S(2)}) collective-permute-start(bf16[128,1024]{1,0:T(8,128)(2,1)} %refs_0_.1), channel_id=1, source_target_pairs={{0,8},{1,9},{2,10},{3,11},{4,12},{5,13},{6,14},{7,15},{8,0},{9,1},... | collective-permute-start | bytes 786440 | tf_op jit(solution)/shard_map/ppermute | solution.py:540
  18.0 16.8 %collective-permute-start.7 = (bf16[4,128,1024]{2,1,0:T(8,128)(2,1)S(1)}, bf16[4,128,1024]{2,1,0:T(8,128)(2,1)S(1)}, u32[]{:S(2)}, u32[]{:S(2)}) collective-permute-start(bf16[4,128,1024]{2,1,0:T(8,128)(2,1)S(1)} %bitcast.96), channel_id=1, source_target_pairs={{0,4},{1,5},{2,6},{3,7},{4,0},{5,1},{6,2},{7,3},{8,12},{9,13},{10,... | collective-permute-start | bytes 3145736 | tf_op jit(solution)/shard_map/ppermute | solution.py:540
  19.0 11.3 %collective-permute-start.6 = (bf16[128,1024]{1,0:T(8,128)(2,1)S(1)}, bf16[128,1024]{1,0:T(8,128)(2,1)S(1)}, u32[]{:S(2)}, u32[]{:S(2)}) collective-permute-start(bf16[128,1024]{1,0:T(8,128)(2,1)S(1)} %dynamic-slice_bitcast_fusion.4), channel_id=1, source_target_pairs={{0,24},{1,25},{2,26},{3,27},{4,28},{5,29},{6,30},{7,31},{8,16},{9,... | collective-permute-start | bytes 786440 | tf_op jit(solution)/shard_map/ppermute | solution.py:540
  21.3 13.5 %collective-permute-start.2 = (bf16[128,1024]{1,0:T(8,128)(2,1)S(1)}, bf16[128,1024]{1,0:T(8,128)(2,1)S(1)}, u32[]{:S(2)}, u32[]{:S(2)}) collective-permute-start(bf16[128,1024]{1,0:T(8,128)(2,1)S(1)} %collective-permute-done.refs_1_), channel_id=1, source_target_pairs={{0,8},{1,9},{2,10},{3,11},{4,12},{5,13},{6,14},{7,15},{8,0},{9,1},... | collective-permute-start | bytes 786440 | tf_op jit(solution)/shard_map/ppermute | solution.py:540
  41.3 16.5 %collective-permute-start.9 = (bf16[2,128,1024]{2,1,0:T(8,128)(2,1)S(1)}, bf16[2,128,1024]{2,1,0:T(8,128)(2,1)S(1)}, u32[]{:S(2)}, u32[]{:S(2)}) collective-permute-start(bf16[2,128,1024]{2,1,0:T(8,128)(2,1)S(1)} %pad_maximum_fusion.4), channel_id=1, source_target_pairs={{0,8},{1,9},{2,10},{3,11},{4,12},{5,13},{6,14},{7,15},{8,0},{9,1},... | collective-permute-start | bytes 1572872 | tf_op jit(solution)/shard_map/ppermute | solution.py:540
  41.4 16.4 %collective-permute-start.10 = (bf16[1,128,1024]{2,1,0:T(8,128)(2,1)S(1)}, bf16[1,128,1024]{2,1,0:T(8,128)(2,1)S(1)}, u32[]{:S(2)}, u32[]{:S(2)}) collective-permute-start(bf16[1,128,1024]{2,1,0:T(8,128)(2,1)S(1)} %bitcast.104), channel_id=1, source_target_pairs={{0,1},{1,0},{2,3},{3,2},{4,6},{5,7},{6,4},{7,5},{8,9},{9,8},{10,11... | collective-permute-start | bytes 786440 | tf_op jit(solution)/shard_map/ppermute | solution.py:540
  57.9 14.7 %collective-permute-start.12 = (bf16[2,1,128,1024]{3,2,1,0:T(8,128)(2,1)S(1)}, bf16[2,1,128,1024]{3,2,1,0:T(8,128)(2,1)S(1)}, u32[]{:S(2)}, u32[]{:S(2)}) collective-permute-start(bf16[2,1,128,1024]{3,2,1,0:T(8,128)(2,1)S(1)} %pad_maximum_fusion.5), channel_id=1, source_target_pairs={{0,2},{1,3},{2,0},{3,1},{4,5},{5,4},{6,7},{7,6},{8,10},{9,11},{10,... | collective-permute-start | bytes 1572872 | tf_op jit(solution)/shard_map/ppermute | solution.py:540
  59.5 13.2 %collective-permute-start.11 = (bf16[2,128,1024]{2,1,0:T(8,128)(2,1)S(1)}, bf16[2,128,1024]{2,1,0:T(8,128)(2,1)S(1)}, u32[]{:S(2)}, u32[]{:S(2)}) collective-permute-start(bf16[2,128,1024]{2,1,0:T(8,128)(2,1)S(1)} %collective-permute-done.9), channel_id=1, source_target_pairs={{0,1},{1,0},{2,3},{3,2},{4,6},{5,7},{6,4},{7,5},{8,9},{9,8},{10,11... | collective-permute-start | bytes 1572872 | tf_op jit(solution)/shard_map/ppermute | solution.py:540
  72.7 15.0 %collective-permute-start.13 = (bf16[2,2,128,1024]{3,2,1,0:T(8,128)(2,1)S(1)}, bf16[2,2,128,1024]{3,2,1,0:T(8,128)(2,1)}, u32[]{:S(2)}, u32[]{:S(2)}) collective-permute-start(bf16[2,2,128,1024]{3,2,1,0:T(8,128)(2,1)S(1)} %pad_maximum_fusion), channel_id=1, source_target_pairs={{0,2},{1,3},{2,0},{3,1},{4,5},{5,4},{6,7},{7,6},{8,10},{9,11},{10,... | collective-permute-start | bytes 3145736 | tf_op jit(solution)/shard_map/ppermute | solution.py:540
  97.6 11.5 %collective-permute-start.17 = (bf16[4,512,1024]{2,1,0:T(8,128)(2,1)}, bf16[4,512,1024]{2,1,0:T(8,128)(2,1)}, u32[]{:S(2)}, u32[]{:S(2)}) collective-permute-start(bf16[4,512,1024]{2,1,0:T(8,128)(2,1)} %get-tuple-element.111), channel_id=1, source_target_pairs={{0,4},{1,5},{2,6},{3,7},{4,0},{5,1},{6,2},{7,3},{8,12},{9,13},{10,... | collective-permute-start | bytes 12582920 | tf_op jit(solution)/shard_map/ppermute | solution.py:540
  97.7 14.6 %collective-permute-start.21 = (bf16[2,2,128,1024]{3,2,1,0:T(8,128)(2,1)}, bf16[2,2,128,1024]{3,2,1,0:T(8,128)(2,1)}, u32[]{:S(2)}, u32[]{:S(2)}) collective-permute-start(bf16[2,2,128,1024]{3,2,1,0:T(8,128)(2,1)} %collective-permute-done.13.refs_6_), channel_id=1, source_target_pairs={{0,4},{1,5},{2,6},{3,7},{4,0},{5,1},{6,2},{7,3},{8,12},{9,13},{10,... | collective-permute-start | bytes 3145736 | tf_op jit(solution)/shard_map/ppermute | solution.py:540
  98.2 14.1 %collective-permute-start.19 = (bf16[2,128,1024]{2,1,0:T(8,128)(2,1)S(1)}, bf16[2,128,1024]{2,1,0:T(8,128)(2,1)S(1)}, u32[]{:S(2)}, u32[]{:S(2)}) collective-permute-start(bf16[2,128,1024]{2,1,0:T(8,128)(2,1)S(1)} %collective-permute-done.9), channel_id=1, source_target_pairs={{0,4},{1,5},{2,6},{3,7},{4,0},{5,1},{6,2},{7,3},{8,12},{9,13},{10,... | collective-permute-start | bytes 1572872 | tf_op jit(solution)/shard_map/ppermute | solution.py:540
  98.3 14.0 %collective-permute-start.20 = (bf16[2,128,1024]{2,1,0:T(8,128)(2,1)S(1)}, bf16[2,128,1024]{2,1,0:T(8,128)(2,1)}, u32[]{:S(2)}, u32[]{:S(2)}) collective-permute-start(bf16[2,128,1024]{2,1,0:T(8,128)(2,1)S(1)} %collective-permute-done.11), channel_id=1, source_target_pairs={{0,4},{1,5},{2,6},{3,7},{4,0},{5,1},{6,2},{7,3},{8,12},{9,13},{10,... | collective-permute-start | bytes 1572872 | tf_op jit(solution)/shard_map/ppermute | solution.py:540
  111.7 39.4 %collective-permute-start.18 = (bf16[2,512,1024]{2,1,0:T(8,128)(2,1)S(1)}, bf16[2,512,1024]{2,1,0:T(8,128)(2,1)}, u32[]{:S(2)}, u32[]{:S(2)}) collective-permute-start(bf16[2,512,1024]{2,1,0:T(8,128)(2,1)S(1)} %add_convert_fusion), channel_id=1, source_target_pairs={{0,1},{1,0},{2,3},{3,2},{4,6},{5,7},{6,4},{7,5},{8,9},{9,8},{10,11... | collective-permute-start | bytes 6291464 | tf_op jit(solution)/shard_map/ppermute | solution.py:540
  154.4 21.4 %collective-permute-start.24 = (bf16[512,1024]{1,0:T(8,128)(2,1)}, bf16[512,1024]{1,0:T(8,128)(2,1)}, u32[]{:S(2)}, u32[]{:S(2)}) collective-permute-start(bf16[512,1024]{1,0:T(8,128)(2,1)} %fusion.4), channel_id=1, source_target_pairs={{0,2},{1,3},{2,0},{3,1},{4,5},{5,4},{6,7},{7,6},{8,10},{9,11},{10,... | collective-permute-start | bytes 3145736 | tf_op jit(solution)/shard_map/ppermute | solution.py:540
  155.6 20.2 %collective-permute-start.23 = (bf16[2,128,1152]{2,1,0:T(8,128)(2,1)S(1)}, bf16[2,128,1152]{2,1,0:T(8,128)(2,1)S(1)}, u32[]{:S(2)}, u32[]{:S(2)}) collective-permute-start(bf16[2,128,1152]{2,1,0:T(8,128)(2,1)S(1)} %add_convert_fusion.2), channel_id=1, source_target_pairs={{0,1},{1,0},{2,3},{3,2},{4,6},{5,7},{6,4},{7,5},{8,9},{9,8},{10,11... | collective-permute-start | bytes 1769480 | tf_op jit(solution)/shard_map/ppermute | solution.py:540
  178.3 13.7 %collective-permute-start.26 = (bf16[256,1024]{1,0:T(8,128)(2,1)S(1)}, bf16[256,1024]{1,0:T(8,128)(2,1)}, u32[]{:S(2)}, u32[]{:S(2)}) collective-permute-start(bf16[256,1024]{1,0:T(8,128)(2,1)S(1)} %fusion.5), channel_id=1, source_target_pairs={{0,8},{1,9},{2,10},{3,11},{4,12},{5,13},{6,14},{7,15},{8,0},{9,1},... | collective-permute-start | bytes 1572872 | tf_op jit(solution)/shard_map/ppermute | solution.py:540
  192.2 13.6 %collective-permute-start.28 = (bf16[4,32,1152]{2,1,0:T(8,128)(2,1)S(1)}, bf16[4,32,1152]{2,1,0:T(8,128)(2,1)S(1)}, u32[]{:S(2)}, u32[]{:S(2)}) collective-permute-start(bf16[4,32,1152]{2,1,0:T(8,128)(2,1)S(1)} %bitcast.114), channel_id=1, source_target_pairs={{0,8},{1,9},{2,10},{3,11},{4,12},{5,13},{6,14},{7,15},{8,0},{9,1},... | collective-permute-start | bytes 884744 | tf_op jit(solution)/shard_map/ppermute | solution.py:540
  195.4 11.6 %collective-permute-start.27 = (bf16[128,1024]{1,0:T(8,128)(2,1)S(1)}, bf16[128,1024]{1,0:T(8,128)(2,1)S(1)}, u32[]{:S(2)}, u32[]{:S(2)}) collective-permute-start(bf16[128,1024]{1,0:T(8,128)(2,1)S(1)} %fusion.9), channel_id=1, source_target_pairs={{0,24},{1,25},{2,26},{3,27},{4,28},{5,29},{6,30},{7,31},{8,16},{9,... | collective-permute-start | bytes 786440 | tf_op jit(solution)/shard_map/ppermute | solution.py:540
  215.3 11.5 %collective-permute-start.30 = (bf16[2,128,1024]{2,1,0:T(8,128)(2,1)S(1)}, bf16[2,128,1024]{2,1,0:T(8,128)(2,1)S(1)}, u32[]{:S(2)}, u32[]{:S(2)}) collective-permute-start(bf16[2,128,1024]{2,1,0:T(8,128)(2,1)S(1)} %pad_maximum_fusion.6), channel_id=1, source_target_pairs={{0,2},{1,3},{2,0},{3,1},{4,5},{5,4},{6,7},{7,6},{8,10},{9,11},{10,... | collective-permute-start | bytes 1572872 | tf_op jit(solution)/shard_map/ppermute | solution.py:540
  219.8 18.8 %collective-permute-start.34 = (bf16[1,4,32,1152]{3,2,1,0:T(8,128)(2,1)S(1)}, bf16[1,4,32,1152]{3,2,1,0:T(8,128)(2,1)S(1)}, u32[]{:S(2)}, u32[]{:S(2)}) collective-permute-start(bf16[1,4,32,1152]{3,2,1,0:T(8,128)(2,1)S(1)} %bitcast.91), channel_id=1, source_target_pairs={{0,4},{1,5},{2,6},{3,7},{4,0},{5,1},{6,2},{7,3},{8,12},{9,13},{10,... | collective-permute-start | bytes 884744 | tf_op jit(solution)/shard_map/ppermute | solution.py:540
  226.4 12.3 %collective-permute-start.35 = (bf16[1,4,32,1152]{3,2,1,0:T(8,128)(2,1)S(1)}, bf16[1,4,32,1152]{3,2,1,0:T(8,128)(2,1)S(1)}, u32[]{:S(2)}, u32[]{:S(2)}) collective-permute-start(bf16[1,4,32,1152]{3,2,1,0:T(8,128)(2,1)S(1)} %bitcast.99), channel_id=1, source_target_pairs={{0,4},{1,5},{2,6},{3,7},{4,0},{5,1},{6,2},{7,3},{8,12},{9,13},{10,... | collective-permute-start | bytes 884744 | tf_op jit(solution)/shard_map/ppermute | solution.py:540
  226.4 9.9 %collective-permute-start.33 = (bf16[2,4,32,1152]{3,2,1,0:T(8,128)(2,1)S(1)}, bf16[2,4,32,1152]{3,2,1,0:T(8,128)(2,1)S(1)}, u32[]{:S(2)}, u32[]{:S(2)}) collective-permute-start(bf16[2,4,32,1152]{3,2,1,0:T(8,128)(2,1)S(1)} %pad_maximum_fusion.3), channel_id=1, source_target_pairs={{0,2},{1,3},{2,0},{3,1},{4,5},{5,4},{6,7},{7,6},{8,10},{9,11},{10,... | collective-permute-start | bytes 1769480 | tf_op jit(solution)/shard_map/ppermute | solution.py:540
  (42 other events, 383.2 us)
